TPU v7x, 32 devices: a whole 2x2x4 slice. The times are simulated.
32 devices in a mesh: tower: 2 (over y), dp: 16 (over z, x, core).
Axes of the slice: x: 2, y: 2, z: 4, core: 2. Of those that a mesh axis runs over, the one named last changes fastest.
Arguments:
- hidden_in: bfloat16 [2, 8192, 768], P('tower', 'dp'), may hold values from -6 to 6
- seg_ids: int32 [16, 512], P('dp'), may hold values from 0 to 3, never falling along the last dimension, each value on 1 to 320 neighbouring positions
- labels: int32 [256], P('dp'), may hold values from 0 to 63
- out_grad: bfloat16 [2, 8192, 768], P('tower', 'dp'), may hold values from -2 to 2
- w_qkv: bfloat16 [2, 768, 2304], P('tower'), may hold values from -0.3125 to 0.3125
- b_query: float32 [2, 768], P('tower'), may hold values from -3 to 3
- b_value: float32 [2, 768], P('tower'), may hold values from -3 to 3
- w_out: bfloat16 [2, 768, 768], P('tower'), may hold values from -0.625 to 0.625
- b_out: float32 [2, 768], P('tower'), may hold values from -3 to 3
- ln1_gain: float32 [2, 768], P('tower'), may hold values from 0.5 to 1.5
- ln1_bias: float32 [2, 768], P('tower'), may hold values from -2 to 2
- w_in: bfloat16 [2, 768, 3072], P('tower'), may hold values from -0.21875 to 0.21875
- b_in: float32 [2, 3072], P('tower'), may hold values from -3 to 3
- w_back: bfloat16 [2, 3072, 768], P('tower'), may hold values from -0.109375 to 0.109375
- b_back: float32 [2, 768], P('tower'), may hold values from -3 to 3
- ln2_gain: float32 [2, 768], P('tower'), may hold values from 0.5 to 1.5
- ln2_bias: float32 [2, 768], P('tower'), may hold values from -2 to 2
Outputs:
- out_hidden: bfloat16 [2, 8192, 768], P('tower', 'dp')
- grad_hidden: bfloat16 [2, 8192, 768], P('tower', 'dp')
- grad_w_qkv: float32 [2, 768, 2304], P('tower', 'dp')
- grad_b_query: float32 [2, 768], P('tower', 'dp')
- grad_b_value: float32 [2, 768], P('tower', 'dp')
- grad_w_out: float32 [2, 768, 768], P('tower', 'dp')
- grad_b_out: float32 [2, 768], P('tower', 'dp')
- grad_ln1_gain: float32 [2, 768], P('tower', 'dp')
- grad_ln1_bias: float32 [2, 768], P('tower', 'dp')
- grad_w_in: float32 [2, 768, 3072], P('tower', 'dp')
- grad_b_in: float32 [2, 3072], P('tower', 'dp')
- grad_w_back: float32 [2, 3072, 768], P('tower', 'dp')
- grad_b_back: float32 [2, 768], P('tower', 'dp')
- grad_ln2_gain: float32 [2, 768], P('tower', 'dp')
- grad_ln2_bias: float32 [2, 768], P('tower', 'dp')
Inputs may be any that keep to these rules, and one draw needn't show every extreme that they name: `seg_ids`: each row holds 4 passages in order, each 1 to 320 tokens long, and one passage of each row has exactly 320.
All inputs are finite; a program needn't handle non-finite values.
Results may differ from a plain program's by a relative error of at most 0.014.
The roundings to bfloat16 on the way count: a program that leaves them out, or rounds other values in their place, can miss the bound.
Values may be sent and summed in bfloat16 or wider, within the bound.
No kernel may reach another device: no remote copies, remote signals or barrier semaphores. Data moves between devices by JAX's collectives and lax.ppermute only.
A program may use at most 192 MiB of HBM per device.

v0:
```python
import math

import jax
import jax.numpy as jnp
from jax import lax
from jax.sharding import PartitionSpec as P

HEAD_DIM = 64
QLEN = 32
SEGS = 4


eps_norm = 1e-05


def shifted_2(value, axis, steps):
    count = lax.axis_size(axis)
    leading, last = (max(0, -steps), min(count, count - steps))
    return lax.ppermute(value, axis, [(source, source + steps) for source in range(leading, last)])


def layer_norm(hidden, norm_gain, norm_bias):
    average = jnp.mean(hidden, -1, keepdims=True)
    centred = hidden - average
    inverse = lax.rsqrt(jnp.mean(centred * centred, -1, keepdims=True) + eps_norm)
    normed = centred * inverse
    return (normed * norm_gain + norm_bias, normed, inverse)


def norm_grad(grad_out, normed, inverse, norm_gain):
    scaled = grad_out * norm_gain
    grad_in = inverse * (
        scaled
        - jnp.mean(scaled, -1, keepdims=True)
        - normed * jnp.mean(scaled * normed, -1, keepdims=True)
    )
    return (grad_in, jnp.sum(grad_out * normed, 0), jnp.sum(grad_out, 0))


def split_heads(proj_low):
    length = proj_low.shape[0]
    model_width = proj_low.shape[1] // 3
    shaped = proj_low.reshape(length, 3, model_width // HEAD_DIM, HEAD_DIM)
    return (shaped[:, 0], shaped[:, 1], shaped[:, 2])


def masked_scores(queries, keys, segment):
    scores = jnp.einsum("qhe,khe->hqk", queries, keys, preferred_element_type=jnp.float32) * (
        1.0 / math.sqrt(queries.shape[-1])
    )
    allowed = segment[:, None] == segment[None, :]
    return jnp.where(allowed[None], scores, -1000000000.0)


def gelu_exact(values):
    return jax.nn.gelu(values, approximate=False)


def contract_rows(left, right):
    return jnp.einsum("ld,le->de", left, right, preferred_element_type=jnp.float32)


def forward_row(row_input, segment, weights):
    (
        w_qkv,
        b_query,
        b_value,
        w_out,
        b_out,
        ln1_gain,
        ln1_bias,
        w_in,
        b_in,
        w_back,
        b_back,
        ln2_gain,
        ln2_bias,
    ) = weights
    length, model_width = row_input.shape
    bias_all = jnp.concatenate([b_query, jnp.zeros_like(b_query), b_value])
    proj_low = (jnp.dot(row_input, w_qkv, preferred_element_type=jnp.float32) + bias_all).astype(
        jnp.bfloat16
    )
    queries, keys, values = split_heads(proj_low)
    scores = masked_scores(queries, keys, segment)
    row_top = jnp.max(scores, -1, keepdims=True)
    shifted = jnp.exp(scores - row_top)
    row_total = jnp.sum(shifted, -1, keepdims=True)
    log_total = row_top + jnp.log(row_total)
    attended = jnp.einsum(
        "hqk,khe->qhe",
        (shifted / row_total).astype(jnp.bfloat16),
        values,
        preferred_element_type=jnp.float32,
    )
    attended_low = attended.reshape(length, model_width).astype(jnp.bfloat16)
    first = row_input.astype(jnp.float32) + (
        jnp.dot(attended_low, w_out, preferred_element_type=jnp.float32) + b_out
    )
    normed_first, normed_one, inverse_one = layer_norm(first, ln1_gain, ln1_bias)
    first_low = normed_first.astype(jnp.bfloat16)
    inner = jnp.dot(first_low, w_in, preferred_element_type=jnp.float32) + b_in
    act_low = gelu_exact(inner).astype(jnp.bfloat16)
    second = normed_first + (jnp.dot(act_low, w_back, preferred_element_type=jnp.float32) + b_back)
    final, normed_two, inverse_two = layer_norm(second, ln2_gain, ln2_bias)
    kept = (
        proj_low,
        log_total,
        attended_low,
        normed_one,
        inverse_one,
        first_low,
        inner,
        act_low,
        normed_two,
        inverse_two,
    )
    return (final, kept)


def ffn_back(grad_final, kept, weights):
    (
        w_qkv,
        b_query,
        b_value,
        w_out,
        b_out,
        ln1_gain,
        ln1_bias,
        w_in,
        b_in,
        w_back,
        b_back,
        ln2_gain,
        ln2_bias,
    ) = weights
    (
        proj_low,
        log_total,
        attended_low,
        normed_one,
        inverse_one,
        first_low,
        inner,
        act_low,
        normed_two,
        inverse_two,
    ) = kept
    grad_second, grad_gain_two, grad_bias_two = norm_grad(
        grad_final, normed_two, inverse_two, ln2_gain
    )
    second_low = grad_second.astype(jnp.bfloat16)
    grad_w_back = contract_rows(act_low, second_low)
    grad_b_back = jnp.sum(second_low.astype(jnp.float32), 0)
    grad_act = jnp.einsum("ld,fd->lf", second_low, w_back, preferred_element_type=jnp.float32)
    unused, gelu_back = jax.vjp(gelu_exact, inner)
    inner_low = gelu_back(grad_act)[0].astype(jnp.bfloat16)
    grad_w_in = contract_rows(first_low, inner_low)
    grad_b_in = jnp.sum(inner_low.astype(jnp.float32), 0)
    grad_normed = grad_second + jnp.einsum(
        "lf,df->ld", inner_low, w_in, preferred_element_type=jnp.float32
    )
    grad_first, grad_gain_one, grad_bias_one = norm_grad(
        grad_normed, normed_one, inverse_one, ln1_gain
    )
    return (
        grad_first,
        (
            grad_w_back,
            grad_b_back,
            grad_w_in,
            grad_b_in,
            grad_gain_two,
            grad_bias_two,
            grad_gain_one,
            grad_bias_one,
        ),
    )


def attention_back(grad_first, row_input, segment, proj_low, log_total, attended_low, weights):
    (
        w_qkv,
        b_query,
        b_value,
        w_out,
        b_out,
        ln1_gain,
        ln1_bias,
        w_in,
        b_in,
        w_back,
        b_back,
        ln2_gain,
        ln2_bias,
    ) = weights
    length, model_width = row_input.shape
    first_grad_low = grad_first.astype(jnp.bfloat16)
    grad_w_out = contract_rows(attended_low, first_grad_low)
    grad_b_out = jnp.sum(first_grad_low.astype(jnp.float32), 0)
    grad_att = jnp.einsum("ld,ed->le", first_grad_low, w_out, preferred_element_type=jnp.float32)
    grad_att = grad_att.astype(jnp.bfloat16).reshape(length, model_width // HEAD_DIM, HEAD_DIM)
    queries, keys, values = split_heads(proj_low)
    scores = masked_scores(queries, keys, segment)
    probabilities = jnp.exp(scores - log_total)
    grad_probs = jnp.einsum("qhe,khe->hqk", grad_att, values, preferred_element_type=jnp.float32)
    grad_values = jnp.einsum(
        "hqk,qhe->khe",
        probabilities.astype(jnp.bfloat16),
        grad_att,
        preferred_element_type=jnp.float32,
    )
    grad_scores = probabilities * (
        grad_probs - jnp.sum(grad_probs * probabilities, -1, keepdims=True)
    )
    scores_low = grad_scores.astype(jnp.bfloat16)
    scale_factor = 1.0 / math.sqrt(HEAD_DIM)
    grad_queries = (
        jnp.einsum("hqk,khe->qhe", scores_low, keys, preferred_element_type=jnp.float32)
        * scale_factor
    )
    grad_keys = (
        jnp.einsum("hqk,qhe->khe", scores_low, queries, preferred_element_type=jnp.float32)
        * scale_factor
    )
    grad_proj = (
        jnp.stack([grad_queries, grad_keys, grad_values], 1)
        .reshape(length, 3 * model_width)
        .astype(jnp.bfloat16)
    )
    column_sums = jnp.sum(grad_proj.astype(jnp.float32), 0)
    grad_w_qkv = contract_rows(row_input, grad_proj)
    grad_input = grad_first + jnp.einsum(
        "le,de->ld", grad_proj, w_qkv, preferred_element_type=jnp.float32
    )
    return (
        grad_input,
        (
            grad_w_qkv,
            column_sums[:model_width],
            column_sums[2 * model_width :],
            grad_w_out,
            grad_b_out,
        ),
    )


def shards(
    hidden_in,
    seg_ids,
    labels,
    out_grad,
    w_qkv,
    b_query,
    b_value,
    w_out,
    b_out,
    ln1_gain,
    ln1_bias,
    w_in,
    b_in,
    w_back,
    b_back,
    ln2_gain,
    ln2_bias,
):
    weights = tuple(
        (
            member[0]
            for member in (
                w_qkv,
                b_query,
                b_value,
                w_out,
                b_out,
                ln1_gain,
                ln1_bias,
                w_in,
                b_in,
                w_back,
                b_back,
                ln2_gain,
                ln2_bias,
            )
        )
    )
    row_count, length = seg_ids.shape
    model_width = hidden_in.shape[2]
    is_query = lax.axis_index("tower") == 0
    position = jnp.arange(length, dtype=jnp.int32)
    segment = jnp.where(is_query, jnp.broadcast_to(position // QLEN, (row_count, length)), seg_ids)
    inputs = hidden_in[0].reshape(row_count, length, model_width)

    def encode_row(row_pair):
        return forward_row(row_pair[0], row_pair[1], weights)

    outputs = lax.map(lambda row_pair: encode_row(row_pair)[0], (inputs, segment))
    query_count = row_count * length // QLEN
    query_cls = outputs.reshape(query_count, QLEN, model_width)[:, 0]
    starts = jnp.sum(
        (seg_ids[:, None, :] < jnp.arange(SEGS, dtype=jnp.int32)[None, :, None]).astype(jnp.int32),
        -1,
    )
    chosen = (position[None, None, :] == starts[:, :, None]).astype(jnp.float32)
    passage_cls = jnp.einsum(
        "rsl,rld->rsd", chosen, outputs, precision=lax.Precision.HIGHEST
    ).reshape(row_count * SEGS, model_width)
    arrived = shifted_2(query_cls.astype(jnp.bfloat16), "tower", 1)
    passages_all = lax.all_gather(passage_cls.astype(jnp.bfloat16), "dp", axis=0, tiled=True)
    score_scale = 2.0 / math.sqrt(model_width)
    arrived_wide = arrived.astype(jnp.float32)
    passages_wide = passages_all.astype(jnp.float32)
    logits = (
        jnp.einsum("qd,pd->qp", arrived, passages_all, preferred_element_type=jnp.float32)
        * score_scale
    )
    row_top = jnp.max(logits, -1, keepdims=True)
    log_sum = row_top + jnp.log(jnp.sum(jnp.exp(logits - row_top), -1, keepdims=True))
    target = (
        labels[:, None] == jnp.arange(passages_all.shape[0], dtype=jnp.int32)[None, :]
    ).astype(jnp.float32)
    grad_logits = jnp.exp(logits - log_sum) - target
    grad_query = (
        jnp.einsum("qp,pd->qd", grad_logits, passages_wide, precision=lax.Precision.HIGHEST)
        * score_scale
    )
    returned = shifted_2(grad_query.astype(jnp.bfloat16), "tower", -1).astype(grad_query.dtype)
    own_passage = lax.psum_scatter(
        jnp.einsum("qp,qd->pd", grad_logits, arrived_wide, precision=lax.Precision.HIGHEST)
        * score_scale,
        "dp",
        scatter_dimension=0,
        tiled=True,
    )
    query_place = jnp.concatenate(
        [returned[:, None, :], jnp.zeros((query_count, QLEN - 1, model_width), jnp.float32)], 1
    )
    query_place = query_place.reshape(row_count, length, model_width)
    passage_place = jnp.einsum(
        "rsl,rsd->rld",
        chosen,
        own_passage.reshape(row_count, SEGS, model_width),
        precision=lax.Precision.HIGHEST,
    )
    grad_final = out_grad[0].astype(jnp.float32).reshape(
        row_count, length, model_width
    ) + jnp.where(is_query, query_place, passage_place)
    kept = lax.map(lambda row_pair: encode_row(row_pair)[1], (inputs, segment))
    ffn_zero = tuple(
        (jnp.zeros(weights[index].shape, jnp.float32) for index in (9, 10, 7, 8, 11, 12, 5, 6))
    )

    def ffn_step(running, members):
        grad_first, parts = ffn_back(members[0], members[1], weights)
        return (jax.tree.map(jnp.add, running, parts), grad_first)

    ffn_sums, first_grads = lax.scan(ffn_step, ffn_zero, (grad_final, kept))
    attention_zero = tuple(
        (jnp.zeros(weights[index].shape, jnp.float32) for index in (0, 1, 2, 3, 4))
    )

    def attention_step(running, members):
        grad_input, parts = attention_back(
            members[0], members[1], members[2], members[3], members[4], members[5], weights
        )
        return (jax.tree.map(jnp.add, running, parts), grad_input)

    attention_sums, input_grads = lax.scan(
        attention_step, attention_zero, (first_grads, inputs, segment, kept[0], kept[1], kept[2])
    )
    all_shares = lax.psum_scatter(ffn_sums + attention_sums, "dp", scatter_dimension=0, tiled=True)
    ffn_shares = all_shares[:8]
    attention_shares = all_shares[8:]
    (
        share_w_back,
        share_b_back,
        share_w_in,
        share_b_in,
        share_gain_two,
        share_bias_two,
        share_gain_one,
        share_bias_one,
    ) = ffn_shares
    share_w_qkv, share_b_query, share_b_value, share_w_out, share_b_out = attention_shares
    out_hidden = outputs.astype(jnp.bfloat16)
    grad_hidden = input_grads.astype(jnp.bfloat16)
    return (
        out_hidden,
        grad_hidden,
        share_w_qkv[None],
        share_b_query[None],
        share_b_value[None],
        share_w_out[None],
        share_b_out[None],
        share_gain_one[None],
        share_bias_one[None],
        share_w_in[None],
        share_b_in[None],
        share_w_back[None],
        share_b_back[None],
        share_gain_two[None],
        share_bias_two[None],
    )


def solution(mesh):
    placed = (
        P("tower", "dp", None),
        P("dp", None),
        P("dp"),
        P("tower", "dp", None),
        P("tower", None, None),
        P("tower", None),
        P("tower", None),
        P("tower", None, None),
        P("tower", None),
        P("tower", None),
        P("tower", None),
        P("tower", None, None),
        P("tower", None),
        P("tower", None, None),
        P("tower", None),
        P("tower", None),
        P("tower", None),
    )
    return jax.shard_map(
        shards,
        mesh=mesh,
        in_specs=placed,
        out_specs=(
            P("tower", "dp", None),
            P("tower", "dp", None),
            P("tower", "dp", None),
            P("tower", "dp"),
            P("tower", "dp"),
            P("tower", "dp", None),
            P("tower", "dp"),
            P("tower", "dp"),
            P("tower", "dp"),
            P("tower", "dp", None),
            P("tower", "dp"),
            P("tower", "dp", None),
            P("tower", "dp"),
            P("tower", "dp"),
            P("tower", "dp"),
        ),
        check_vma=False,
    )
```

profile of v0, /device:TPU:0, one launch (start us, length us, event | category | flops | bytes accessed | tf_op | source)
XLA Modules:
  0.0 660.2 jit_solution(11464728748658017476)
XLA Ops:
  9.0 1.3 reduce.8
  11.0 1.3 reduce.4
  12.2 1.3 reduce.5
  13.5 1.3 reduce.6
  14.8 1.3 reduce.9
  17.8 4.5 fusion.20
  22.3 4.3 copy.61
  26.6 3.5 fusion.21
  30.1 3.7 fusion
  34.7 4.9 fusion.37
  41.0 20.4 %multiply_convert_fusion.1 = (bf16[512,3072]{1,0:T(8,128)(2,1)S(1)}, f32[512,3072]{1,0:T(8,128)}, f32[512,3072]{1,0:T(8,128)}) fusion(f32[3072]{0:T(1024)S(1)} %bitcast.169, bf16[1,768,3072]{2,1,0:T(8,128)(2,1)} %param.28, f32[512,768]{1,0:T(8,128)S(1)} %get-tuple-element.339, f32[768]{0:T(1024)S(1)} %copy-done.25, f32[768]{0:T(1024)S(1)} %reduce.7, ...), kind=kOutput, calls=%fused_computation.14 | convolution fusion | flops 2521694208 | bytes 22042624 | tf_op jit(solution)/shard_map/while/body/eval_jaxpr/dot_general | solution.py:102
  61.5 2.8 fusion.89
  65.6 6.1 collective-permute-start
  73.4 23.3 %all-gather = bf16[16,4,768]{2,1,0:T(4,128)(2,1)} all-gather(bf16[1,4,768]{2,1,0:T(4,128)(2,1)S(1)} %fusion.53), channel_id=1, replica_groups=mesh['tower'=2,'dp'=16] {'dp'}, dimensions={0}, use_global_device_ids=true | all-gather | bytes 104448 | tf_op jit(solution)/shard_map/all_gather | solution.py:309
  96.7 1.6 reshape.328
  101.5 1.8 fusion.51
  103.3 1.3 collective-permute-start.1
  104.6 1.8 convolution_multiply_fusion
  106.5 2.9 collective-permute-done.1
  110.2 2.1 copy.64
  112.3 82.8 %all-reduce.14.cloned.1.call-done = f32[64,768]{1,0:T(8,128)} async-done(((f32[64,768]{1,0:T(8,128)}), f32[64,768]{1,0:T(8,128)}) %all-reduce.14.cloned.1.call-update) | async-done | bytes 196624
  195.1 4.6 multiply_reduce_fusion.1
  200.8 10.4 %convert_reduce_fusion = (f32[3072]{0:T(1024)}, bf16[512,3072]{1,0:T(8,128)(2,1)S(1)}) fusion(f32[512,3072]{1,0:T(8,128)} %get-tuple-element.333, bf16[1,3072,768]{2,1,0:T(8,128)(2,1)} %param.30, f32[512,768]{1,0:T(8,128)S(1)} %get-tuple-element.327, f32[512,3072]{1,0:T(8,128)} %get-tuple-element.340, f32[3072]{0:T(1024)S(1)} %bitcast.170), kind=kOutput, calls=%fused_computation.11 | convolution fusion | flops 2443047936 | bytes 22044672 | tf_op jit(solution)/shard_map/while/body/eval_jaxpr/ld,fd->lf/dot_general | solution.py:155
  211.3 3.7 multiply_reduce_fusion.2
  217.2 1.7 convolution_convert_fusion
  218.9 2.3 copy.65
  221.2 8.1 %fusion.41 = bf16[512,1,12,64]{0,3,2,1:T(8,128)(2,1)S(1)} fusion(bf16[512,12,64]{0,2,1:T(8,128)(2,1)} %bitcast.154, f32[12,512]{1,0:T(8,128)} %log_add_fusion, f32[12,512,512]{1,2,0:T(8,128)} %copy-done.1, pred[512,512]{0,1:T(8,128)(4,1)} %broadcast_compare_fusion), kind=kOutput, calls=%fused_computation.76 | convolution fusion | flops 415629312 | bytes 14442496 | tf_op jit(solution)/shard_map/while/body/eval_jaxpr/hqk,qhe->khe/dot_general | solution.py:207
  229.3 9.6 %multiply_reduce_fusion = (f32[12,512]{1,0:T(8,128)S(1)}, f32[12,512,512]{1,2,0:T(8,128)}) fusion(f32[12,512]{1,0:T(8,128)S(1)} %copy-done.16, f32[12,512,512]{1,2,0:T(8,128)} %copy-done.1, pred[512,512]{0,1:T(8,128)(4,1)S(1)} %copy-done.6, bf16[512,12,64]{0,2,1:T(8,128)(2,1)S(1)} %bitcast.155, bf16[512,3,12,64]{0,3,2,1:T(8,128)(2,1)} %bitcast.148), kind=kOutput, calls=%fused_computation.1 | convolution fusion | flops 418375680 | bytes 27049984 | tf_op jit(solution)/shard_map/while/body/eval_jaxpr/qhe,khe->hqk/dot_general | solution.py:206
  239.0 7.3 %multiply_convert_fusion = bf16[12,512,512]{1,2,0:T(8,128)(2,1)S(1)} fusion(f32[12,512,512]{1,2,0:T(8,128)} %get-tuple-element.348, f32[12,512]{1,0:T(8,128)S(1)} %get-tuple-element.347, f32[12,512]{1,0:T(8,128)S(1)} %copy-done.16, f32[12,512,512]{1,2,0:T(8,128)S(1)} %bitcast.145, pred[512,512]{0,1:T(8,128)(4,1)S(1)} %copy-done.6), kind=kLoop, calls=%fused_computation | loop fusion | flops 18874368 | bytes 31768576 | tf_op jit(solution)/shard_map/while/body/eval_jaxpr/convert_element_type | solution.py:216
  246.3 2.0 fusion.48
  250.5 1.4 copy-done.5
  251.9 5.0 convolution_bitcast_fusion
  256.8 8.0 %copy.74 = f32[768,2304]{1,0:T(8,128)} copy(f32[768,2304]{0,1:T(8,128)} %convolution_bitcast_fusion) | data formatting | bytes 14155776
  264.9 3.8 fusion.73
  268.8 9.4 %fusion.83 = f32[768,3072]{1,0:T(8,128)} fusion(bf16[512,3072]{1,0:T(8,128)(2,1)} %copy-done.32, f32[512,768]{1,0:T(8,128)} %copy-done.8, f32[768]{0:T(1024)} %reduce.8, f32[768]{0:T(1024)} %copy-done.19, f32[512]{0:T(512)} %copy-done.21, f32[512]{0:T(512)} %copy-done.17), kind=kOutput, calls=%fused_computation.151 | convolution fusion | flops 2417885184 | bytes 14166016 | tf_op jit(solution)/shard_map/while/body/eval_jaxpr/ld,le->de/dot_general | solution.py:60
  278.3 9.1 %fusion.76 = f32[3072,768]{1,0:T(8,128)} fusion(bf16[512,3072]{1,0:T(8,128)(2,1)} %copy-done.12, f32[512,768]{1,0:T(8,128)} %copy-done.7), kind=kOutput, calls=%fused_computation.144 | convolution fusion | flops 2416312320 | bytes 14155776 | tf_op jit(solution)/shard_map/while/body/eval_jaxpr/ld,le->de/dot_general | solution.py:60
  288.7 2.6 fusion.107
  292.7 63.4 %all-reduce.11 = (f32[768]{0:T(1024)}, f32[768]{0:T(1024)}, f32[768]{0:T(1024)}, f32[768]{0:T(1024)}, f32[768]{0:T(1024)}, /*index=5*/f32[3072]{0:T(1024)}, f32[...) all-reduce(f32[768]{0:T(1024)S(1)} %slice.47, ...), channel_id=4, replica_groups=mesh['tower'=2,'dp'=16] {'dp'}, use_global_device_ids=true, to_apply=%region_17.18.clone | all-reduce | flops 9216 | bytes 73728
  356.1 1.3 dynamic-slice.24
  357.5 1.3 dynamic-slice_bitcast_fusion.7
  358.7 1.3 dynamic-slice_bitcast_fusion.6
  362.5 1.3 dynamic-slice_bitcast_fusion.3
  365.5 5.2 fusion.44
  370.7 2.4 copy.75
  373.1 2.4 copy.69
  375.6 46.7 %reduce-scatter.7.cloned.1.call-done = f32[48,768]{1,0:T(8,128)} async-done(((f32[768,768]{1,0:T(8,128)}), f32[48,768]{1,0:T(8,128)}) %reduce-scatter.7.cloned.1.call-update) | async-done | bytes 147472 | tf_op jit(solution)/shard_map/reduce_scatter | solution.py:371
  422.3 115.0 %reduce-scatter.9.cloned.1.call-done = f32[48,3072]{1,0:T(8,128)} async-done(((f32[768,3072]{1,0:T(8,128)}), f32[48,3072]{1,0:T(8,128)}) %reduce-scatter.9.cloned.1.call-update) | async-done | bytes 589840 | tf_op jit(solution)/shard_map/reduce_scatter | solution.py:371
  537.2 116.2 %reduce-scatter.11.cloned.1.call-done = f32[192,768]{1,0:T(8,128)} async-done(((f32[3072,768]{1,0:T(8,128)}), f32[192,768]{1,0:T(8,128)}) %reduce-scatter.11.cloned.1.call-update) | async-done | bytes 589840 | tf_op jit(solution)/shard_map/reduce_scatter | solution.py:371
  (134 shorter events, 24.3 us)
Async XLA Ops:
  7.2 10.6 %copy-start = (bf16[1,768,2304]{2,1,0:T(8,128)(2,1)S(1)}, bf16[1,768,2304]{2,1,0:T(8,128)(2,1)}, u32[]{:S(2)}) copy-start(bf16[1,768,2304]{2,1,0:T(8,128)(2,1)} %param.21) | copy-start | bytes 10616836
  7.2 187.9 %all-reduce.14.cloned.1.call-start = ((), (), s32[]{:S(2)}) async-start(), calls=%async_computation.8 | async-start | bytes 393216
  8.1 53.3 %copy-start.19 = (f32[768]{0:T(1024)}, f32[768]{0:T(1024)S(1)}, u32[]{:S(2)}) copy-start(f32[768]{0:T(1024)S(1)} %reduce.7) | copy-start | bytes 9220
  30.1 4.6 copy-start.1
  34.7 4.9 copy-start.14
  34.7 4.9 copy-start.27
  34.7 4.9 copy-start.28
  39.6 1.4 copy-start.13
  39.6 1.4 copy-start.25
  39.6 1.4 copy-start.30
  39.6 21.8 %slice-start.3 = ((s8[4718592]{0:T(1024)(128)(4,1)}), s8[4194304]{0:T(1024)(128)(4,1)S(1)}, s32[]{:S(2)}) async-start(s8[4718592]{0:T(1024)(128)(4,1)} %bitcast.162), calls=%async_computation.12 | async-start | bytes 8388608
  40.6 20.8 %copy-start.8 = (f32[512,768]{1,0:T(8,128)}, f32[512,768]{1,0:T(8,128)S(1)}, u32[]{:S(2)}) copy-start(f32[512,768]{1,0:T(8,128)S(1)} %get-tuple-element.339) | copy-start | bytes 4718596
  40.6 20.8 %copy-start.17 = (f32[512]{0:T(512)}, f32[512]{0:T(512)S(1)}, u32[]{:S(2)}) copy-start(f32[512]{0:T(512)S(1)} %broadcast_multiply_fusion.5) | copy-start | bytes 6148
  40.9 20.5 %copy-start.21 = (f32[512]{0:T(512)}, f32[512]{0:T(512)S(1)}, u32[]{:S(2)}) copy-start(f32[512]{0:T(512)S(1)} %add_rsqrt_fusion.1) | copy-start | bytes 6148
  41.0 20.5 %copy-start.26 = (f32[768]{0:T(1024)S(1)}, f32[768]{0:T(1024)}, u32[]{:S(2)}) copy-start(f32[768]{0:T(1024)} %reduce.9) | copy-start | bytes 9220
  41.0 20.5 %slice-start.4 = ((s8[4718592]{0:T(1024)(128)(4,1)}), s8[524288]{0:T(1024)(128)(4,1)S(1)}, s32[]{:S(2)}) async-start(s8[4718592]{0:T(1024)(128)(4,1)} %bitcast.162), calls=%async_computation.13 | async-start | bytes 1048576
  61.4 2.9 copy-start.12
  64.3 8.2 %copy-start.2 = (f32[512,768]{1,0:T(8,128)}, f32[512,768]{1,0:T(8,128)S(1)}, u32[]{:S(2)}) copy-start(f32[512,768]{1,0:T(8,128)S(1)} %get-tuple-element.342) | copy-start | bytes 4718596
  64.3 8.1 %copy-start.23 = (s32[1,512]{1,0:T(1,128)S(1)}, s32[1,512]{1,0:T(1,128)}, u32[]{:S(2)}) copy-start(s32[1,512]{1,0:T(1,128)} %param.18) | copy-start | bytes 6148
  65.6 34.6 %collective-permute-start = (bf16[16,768]{1,0:T(8,128)(2,1)}, bf16[16,768]{1,0:T(8,128)(2,1)}, u32[]{:S(2)}, u32[]{:S(2)}) collective-permute-start(bf16[16,768]{1,0:T(8,128)(2,1)} %bitcast.143), channel_id=1, source_target_pairs={{0,16},{1,17},{2,18},{3,19},{4,20},{5,21},{6,22},{7,23},{8,24},{9,... | collective-permute-start | bytes 73736 | tf_op jit(solution)/shard_map/ppermute | solution.py:19
  72.5 0.9 copy-start.24
  103.3 6.0 collective-permute-start.1
  106.4 264.3 %reduce-scatter.13.cloned.1.call-start = ((), (), s32[]{:S(2)}) async-start(), calls=%async_computation.7 | async-start | bytes 7520256
  195.1 4.6 copy-start.3
  199.7 1.1 copy-start.31
  199.7 11.5 %slice-start.5 = ((s8[4718592]{0:T(1024)(128)(4,1)}), s8[4194304]{0:T(1024)(128)(4,1)S(1)}, s32[]{:S(2)}) async-start(s8[4718592]{0:T(1024)(128)(4,1)} %bitcast.164), calls=%async_computation.14 | async-start | bytes 8388608
  200.8 10.4 %copy-start.7 = (f32[512,768]{1,0:T(8,128)}, f32[512,768]{1,0:T(8,128)S(1)}, u32[]{:S(2)}) copy-start(f32[512,768]{1,0:T(8,128)S(1)} %get-tuple-element.327) | copy-start | bytes 4718596
  200.8 10.4 %copy-start.9 = (f32[512,768]{1,0:T(8,128)S(1)}, f32[512,768]{1,0:T(8,128)}, u32[]{:S(2)}) copy-start(f32[512,768]{1,0:T(8,128)} %copy-done.8) | copy-start | bytes 4718596
  200.8 10.4 %copy-start.18 = (f32[512]{0:T(512)S(1)}, f32[512]{0:T(512)}, u32[]{:S(2)}) copy-start(f32[512]{0:T(512)} %copy-done.17) | copy-start | bytes 6148
  200.8 10.4 %copy-start.20 = (f32[768]{0:T(1024)S(1)}, f32[768]{0:T(1024)}, u32[]{:S(2)}) copy-start(f32[768]{0:T(1024)} %copy-done.19) | copy-start | bytes 9220
  200.8 10.4 %copy-start.22 = (f32[512]{0:T(512)S(1)}, f32[512]{0:T(512)}, u32[]{:S(2)}) copy-start(f32[512]{0:T(512)} %copy-done.21) | copy-start | bytes 6148
  200.8 10.4 %slice-start.6 = ((s8[4718592]{0:T(1024)(128)(4,1)}), s8[524288]{0:T(1024)(128)(4,1)S(1)}, s32[]{:S(2)}) async-start(s8[4718592]{0:T(1024)(128)(4,1)} %bitcast.164), calls=%async_computation.15 | async-start | bytes 1048576
  211.2 3.7 copy-start.32
  214.9 2.2 copy-start.29
  216.0 1.1 copy-start.10
  221.2 8.1 %copy-start.6 = (pred[512,512]{0,1:T(8,128)(4,1)S(1)}, pred[512,512]{0,1:T(8,128)(4,1)}, u32[]{:S(2)}) copy-start(pred[512,512]{0,1:T(8,128)(4,1)} %broadcast_compare_fusion) | copy-start | bytes 786436
  221.2 8.1 %copy-start.11 = (bf16[512,768]{0,1:T(8,128)(2,1)S(1)}, bf16[512,768]{0,1:T(8,128)(2,1)}, u32[]{:S(2)}) copy-start(bf16[512,768]{0,1:T(8,128)(2,1)} %copy.65) | copy-start | bytes 2359300
  221.2 8.1 %copy-start.16 = (f32[12,512]{1,0:T(8,128)S(1)}, f32[12,512]{1,0:T(8,128)}, u32[]{:S(2)}) copy-start(f32[12,512]{1,0:T(8,128)} %log_add_fusion) | copy-start | bytes 73732
  221.2 17.8 %slice-start = ((s8[12582912]{0:T(1024)(128)(4,1)}), s8[4194304]{0:T(1024)(128)(4,1)S(1)}, s32[]{:S(2)}) async-start(s8[12582912]{0:T(1024)(128)(4,1)} %bitcast.144), calls=%async_computation.9 | async-start | bytes 8388608
  221.2 17.8 %slice-start.1 = ((s8[12582912]{0:T(1024)(128)(4,1)}), s8[4194304]{0:T(1024)(128)(4,1)S(1)}, s32[]{:S(2)}) async-start(s8[12582912]{0:T(1024)(128)(4,1)} %bitcast.144), calls=%async_computation.10 | async-start | bytes 8388608
  229.3 9.7 %slice-start.2 = ((s8[12582912]{0:T(1024)(128)(4,1)}), s8[4194304]{0:T(1024)(128)(4,1)S(1)}, s32[]{:S(2)}) async-start(s8[12582912]{0:T(1024)(128)(4,1)} %bitcast.144), calls=%async_computation.11 | async-start | bytes 8388608
  239.0 7.3 %copy-start.4 = (bf16[512,2304]{0,1:T(8,128)(2,1)S(1)}, bf16[512,2304]{0,1:T(8,128)(2,1)}, u32[]{:S(2)}) copy-start(bf16[512,2304]{0,1:T(8,128)(2,1)} %copy.61) | copy-start | bytes 7077892
  249.4 2.4 copy-start.15
  250.5 1.4 copy-start.5
  264.9 157.4 %reduce-scatter.7.cloned.1.call-start = ((), (), s32[]{:S(2)}) async-start(), calls=%async_computation.4 | async-start | bytes 2506752 | tf_op jit(solution)/shard_map/reduce_scatter | solution.py:371
  268.8 268.5 %reduce-scatter.9.cloned.1.call-start = ((), (), s32[]{:S(2)}) async-start(), calls=%async_computation.5 | async-start | bytes 10027008 | tf_op jit(solution)/shard_map/reduce_scatter | solution.py:371
  278.3 375.2 %reduce-scatter.11.cloned.1.call-start = ((), (), s32[]{:S(2)}) async-start(), calls=%async_computation.6 | async-start | bytes 10027008 | tf_op jit(solution)/shard_map/reduce_scatter | solution.py:371
Sparse Core Ops, SparseCore 0:
  106.5 88.5 all-reduce.13
  265.0 89.7 reduce-scatter.12
  359.6 62.6 reduce-scatter.6
  426.8 110.3 reduce-scatter.8
  542.3 111.1 reduce-scatter.10
where the time goes:
time: 671 us; the launch traced here: 660 us
  waiting for transfers between devices  364 us (54%)
  matrix products  116 us (17%)
  blocking collectives  86.7 us (13%)
  local copies, waits for them, and re-layouts  39.3 us (6%)
  other arithmetic  30.1 us (4%)
  between operations  16.5 us (2%)
  starting transfers between devices  7.63 us (1%)
    reduce_scatter x3, waiting for transfers between devices, shards(): lax.psum_scatter(ffn_sums + attention_sums, 'dp', scatter_dimension=0, ti...  278 us
    unnamed x7, waiting for transfers between devices  82.9 us
    unnamed x1, blocking collectives  63.4 us
    dot_general x4, matrix products, contract_rows(): jnp.einsum('ld,le->de', left, right, preferred_element_type=jnp.float32)  27.3 us
    all_gather x1, blocking collectives, shards(): lax.all_gather(passage_cls.astype(jnp.bfloat16), 'dp', axis=0, tiled=True)  23.3 us
    unnamed x87, local copies, waits for them, and re-layouts  21.1 us
    dot_general x1, matrix products, forward_row(): inner = jnp.dot(first_low, w_in, preferred_element_type=jnp.float32) + b_in  20.4 us
  transfers between devices with their start and end apart: 7, of which 5 were waited for; matrix products, arithmetic and copies ran while one was open for 8% of the time, Pallas kernels for 0%

commit v1 on v0

v1 whole, which is shorter than its diff:
```python
import functools
import math

import jax
import jax.numpy as jnp
from jax import lax
from jax.experimental import pallas as pl
from jax.experimental.pallas import tpu as pltpu
from jax.sharding import PartitionSpec as P

HEAD_DIM = 64
QLEN = 32
SEGS = 4
PACKET = 24
EPS = 1e-05
BF = jnp.bfloat16
F32 = jnp.float32
TILE = 32

VM = pl.BlockSpec(memory_space=pltpu.VMEM)
SM = pl.BlockSpec(memory_space=pltpu.SMEM)


def nn(a, b):
    return lax.dot_general(a, b, (((1,), (0,)), ((), ())), preferred_element_type=F32)


def nt(a, b):
    return lax.dot_general(a, b, (((1,), (1,)), ((), ())), preferred_element_type=F32)


def tn(a, b):
    return lax.dot_general(a, b, (((0,), (0,)), ((), ())), preferred_element_type=F32)


def kernel_call(body, outs, args, scratch=(), smem=0, mib=32, flops=0, name=None):
    single = not isinstance(outs, (list, tuple))
    shapes = [outs] if single else list(outs)
    moved = sum(math.prod(a.shape) * a.dtype.itemsize for a in list(args) + shapes)
    result = pl.pallas_call(
        body,
        out_shape=shapes,
        in_specs=[SM] * smem + [VM] * (len(args) - smem),
        out_specs=[VM] * len(shapes),
        scratch_shapes=list(scratch),
        compiler_params=pltpu.CompilerParams(vmem_limit_bytes=mib << 20),
        cost_estimate=pl.CostEstimate(flops=flops, bytes_accessed=moved, transcendentals=0),
        name=name,
    )(*args)
    return result[0] if single else result


def sds(shape, dtype):
    return jax.ShapeDtypeStruct(shape, dtype)


def fold(value):
    rows, cols = value.shape
    return jnp.sum(value.reshape(rows // 8, 8, cols), 0)


def head_mask(half):
    lane = lax.broadcasted_iota(jnp.int32, (1, 2 * HEAD_DIM), 1)
    return (lane // HEAD_DIM == half).astype(F32).astype(BF)


def normalise(value):
    centred = value - jnp.mean(value, -1, keepdims=True)
    inverse = lax.rsqrt(jnp.mean(centred * centred, -1, keepdims=True) + EPS)
    return centred * inverse, inverse


def norm_back(grad, normed, inverse, gain):
    scaled = grad * gain
    return inverse * (
        scaled
        - jnp.mean(scaled, -1, keepdims=True)
        - normed * jnp.mean(scaled * normed, -1, keepdims=True)
    )


def gelu_pair(value):
    cdf = 0.5 * lax.erf(value * (1.0 / math.sqrt(2.0))) + 0.5
    density = jnp.exp(value * value * -0.5) * (1.0 / math.sqrt(2.0 * math.pi))
    return value * cdf, cdf + value * density


def proj_kernel(x, w, bq, bv, out):
    width = x.shape[1]
    for part in range(3):
        cols = slice(part * width, (part + 1) * width)
        value = nn(x[...], w[:, cols])
        if part == 0:
            value = value + bq[...]
        if part == 2:
            value = value + bv[...]
        out[:, cols] = value.astype(BF)


def chosen_rows(tower, seg, count, length):
    row = lax.broadcasted_iota(jnp.int32, (count, 1), 0)
    place = lax.broadcasted_iota(jnp.int32, (count, length), 1)
    start = jnp.sum((seg < row).astype(F32), 1, keepdims=True).astype(jnp.int32)
    wanted = jnp.where(tower == 0, row * QLEN, jnp.where(row < SEGS, start, -1))
    return (place == wanted).astype(F32)


def cls_kernel(place, seg, x, proj, w_out, b_out, g1, b1, w_in, b_in, w_back, b_back, g2, b2, cls):
    length, width = x.shape
    count = cls.shape[0]
    heads = width // HEAD_DIM
    tower = place[0]
    pick = chosen_rows(tower, seg[...], count, length)
    pick_low = pick.astype(BF)
    x_cls = nn(pick_low, x[...])
    q_cls = (nn(pick_low, proj[:, :width]) * (1.0 / math.sqrt(HEAD_DIM))).astype(BF)
    place_row = lax.broadcasted_iota(jnp.int32, (1, length), 1)
    own_seg = jnp.where(tower == 0, place_row // QLEN, seg[...])
    row = lax.broadcasted_iota(jnp.int32, (count, 1), 0)
    bias = jnp.where(own_seg == row, 0.0, -1e9)
    lane_head = lax.broadcasted_iota(jnp.int32, (1, width), 1) // HEAD_DIM
    spread = jnp.concatenate(
        [q_cls * (lane_head == h).astype(F32).astype(BF) for h in range(heads)], 0
    )
    scores = nt(spread, proj[:, width : 2 * width]) + jnp.concatenate([bias] * heads, 0)
    shifted = jnp.exp(scores - jnp.max(scores, -1, keepdims=True))
    probs = (shifted / jnp.sum(shifted, -1, keepdims=True)).astype(BF)
    mixed = nn(probs, proj[:, 2 * width :])
    attended = jnp.zeros((count, width), F32)
    for h in range(heads):
        attended = attended + jnp.where(lane_head == h, mixed[h * count : (h + 1) * count], 0.0)
    first = x_cls + (nn(attended.astype(BF), w_out[...]) + b_out[...])
    normed = normalise(first)[0] * g1[...] + b1[...]
    inner = nn(normed.astype(BF), w_in[...]) + b_in[...]
    act = gelu_pair(inner)[0].astype(BF)
    second = normed + (nn(act, w_back[...]) + b_back[...])
    final = normalise(second)[0] * g2[...] + b2[...]
    cls[...] = final.astype(BF)


def attention_kernel(place, seg_row, seg_col, proj, attended, probs, bias_scratch):
    length = proj.shape[0]
    width = proj.shape[1] // 3
    tower = place[0]
    lane = lax.broadcasted_iota(jnp.int32, (1, length), 1)
    sub = lax.broadcasted_iota(jnp.int32, (length, 1), 0)
    row_seg = jnp.where(tower == 0, lane // QLEN, seg_row[...])
    col_seg = jnp.where(tower == 0, sub // QLEN, seg_col[...])
    bias_scratch[...] = jnp.where(col_seg == row_seg, 0.0, -1e9)
    masks = [head_mask(0), head_mask(1)]
    scale = 1.0 / math.sqrt(HEAD_DIM)
    pair_width = 2 * HEAD_DIM

    def pair_step(pair, carry):
        at = pl.multiple_of(pair * pair_width, pair_width)
        queries = proj[:, pl.ds(at, pair_width)] * jnp.asarray(scale, BF)
        keys = proj[:, pl.ds(pl.multiple_of(width + at, pair_width), pair_width)]
        values = proj[:, pl.ds(pl.multiple_of(2 * width + at, pair_width), pair_width)]
        mixed = None
        for half in range(2):
            scores = nt(queries * masks[half], keys) + bias_scratch[...]
            shifted = jnp.exp(scores - jnp.max(scores, -1, keepdims=True))
            total = jnp.sum(shifted, -1, keepdims=True)
            low = (shifted * (1.0 / total)).astype(BF)
            probs[2 * pair + half] = low
            term = nn(low, values * masks[half])
            mixed = term if mixed is None else mixed + term
        attended[:, pl.ds(at, pair_width)] = mixed.astype(BF)
        return carry

    lax.fori_loop(0, width // pair_width, pair_step, 0)


def first_kernel(x, attended, w_out, b_out, g1, b1, n1, r1, low, work):
    work[...] = nn(attended[...], w_out[...])

    def step(i, carry):
        rows = pl.ds(pl.multiple_of(i * TILE, TILE), TILE)
        first = x[rows, :].astype(F32) + (work[rows, :] + b_out[...])
        normed, inverse = normalise(first)
        n1[rows, :] = normed
        r1[rows, :] = inverse
        low[rows, :] = (normed * g1[...] + b1[...]).astype(BF)
        return carry

    lax.fori_loop(0, x.shape[0] // TILE, step, 0)


def inner_kernel(low, w_in, b_in, act, slope, work):
    length = low.shape[0]
    block = work.shape[2]
    blocks = w_in.shape[1] // block
    work[0] = nn(low[...], w_in[:, :block])

    def gelu_block(i, slot):
        cols = pl.ds(pl.multiple_of(i * block, block), block)
        bias = b_in[:, cols]
        for r in range(0, length, TILE):
            value, grad = gelu_pair(work[slot, r : r + TILE, :] + bias)
            act[r : r + TILE, cols] = value.astype(BF)
            slope[r : r + TILE, cols] = grad.astype(BF)

    def step(i, carry):
        slot = lax.rem(i, 2)
        later = pl.ds(pl.multiple_of((i + 1) * block, block), block)
        work[1 - slot] = nn(low[...], w_in[:, later])
        gelu_block(i, slot)
        return carry

    lax.fori_loop(0, blocks - 1, step, 0)
    gelu_block(blocks - 1, (blocks - 1) % 2)


def second_kernel(act, w_back, b_back, n1, g1, b1, g2, b2, n2, r2, out, work):
    work[...] = nn(act[...], w_back[...])

    def step(i, carry):
        rows = pl.ds(pl.multiple_of(i * TILE, TILE), TILE)
        second = (n1[rows, :] * g1[...] + b1[...]) + (work[rows, :] + b_back[...])
        normed, inverse = normalise(second)
        n2[rows, :] = normed
        r2[rows, :] = inverse
        out[rows, :] = (normed * g2[...] + b2[...]).astype(BF)
        return carry

    lax.fori_loop(0, act.shape[0] // TILE, step, 0)


def loss_kernel(place, queries, passages, labels_row, labels_col, grad):
    tower, index = place[0], place[1]
    total_q, width = queries.shape
    total_p = passages.shape[0]
    count = grad.shape[0]
    scale = 2.0 / math.sqrt(width)
    own = (
        lax.broadcasted_iota(jnp.int32, (count, total_q), 1)
        == lax.broadcasted_iota(jnp.int32, (count, total_q), 0) + index * count
    )
    own_q = nn(own.astype(F32).astype(BF), queries[...]).astype(BF)
    logits = nt(own_q, passages[...]) * scale
    peak = jnp.max(logits, -1, keepdims=True)
    soft = jnp.exp(logits - peak)
    soft = soft / jnp.sum(soft, -1, keepdims=True)
    own_label = jnp.sum(
        jnp.where(own, labels_row[...].astype(F32), 0.0), 1, keepdims=True
    ).astype(jnp.int32)
    hit = lax.broadcasted_iota(jnp.int32, (count, total_p), 1) == own_label
    grad_logits = soft - hit.astype(F32)
    wide_p = passages[...].astype(F32)
    grad_q = (
        jnp.dot(grad_logits, wide_p, precision=lax.Precision.HIGHEST, preferred_element_type=F32)
        * scale
    )
    every = nt(queries[...], passages[...]) * scale
    peak = jnp.max(every, -1, keepdims=True)
    soft = jnp.exp(every - peak)
    soft = soft / jnp.sum(soft, -1, keepdims=True)
    hit = lax.broadcasted_iota(jnp.int32, (total_q, total_p), 1) == labels_col[...]
    every_grad = soft - hit.astype(F32)
    mine = jnp.logical_and(
        lax.broadcasted_iota(jnp.int32, (count, total_p), 1)
        == lax.broadcasted_iota(jnp.int32, (count, total_p), 0) + index * SEGS,
        lax.broadcasted_iota(jnp.int32, (count, total_p), 0) < SEGS,
    ).astype(F32)
    picked = lax.dot_general(
        mine, every_grad, (((1,), (1,)), ((), ())),
        precision=lax.Precision.HIGHEST, preferred_element_type=F32,
    )
    grad_p = (
        jnp.dot(
            picked, queries[...].astype(F32),
            precision=lax.Precision.HIGHEST, preferred_element_type=F32,
        )
        * scale
    )
    grad[...] = jnp.where(tower == 0, grad_q, grad_p)


def second_back_kernel(place, seg, out_grad, cls_grad, n2, r2, g2, grad, low, sums, work):
    length, width = out_grad.shape
    count = cls_grad.shape[0]
    pick = chosen_rows(place[0], seg[...], count, length)
    work[...] = lax.dot_general(
        pick, cls_grad[...], (((0,), (0,)), ((), ())),
        precision=lax.Precision.HIGHEST, preferred_element_type=F32,
    )

    def step(i, carry):
        gain_sum, bias_sum, low_sum = carry
        rows = pl.ds(pl.multiple_of(i * TILE, TILE), TILE)
        final = out_grad[rows, :].astype(F32) + work[rows, :]
        normed = n2[rows, :]
        back = norm_back(final, normed, r2[rows, :], g2[...])
        grad[rows, :] = back
        back_low = back.astype(BF)
        low[rows, :] = back_low
        return (
            gain_sum + fold(final * normed),
            bias_sum + fold(final),
            low_sum + fold(back_low.astype(F32)),
        )

    zero = jnp.zeros((8, width), F32)
    parts = lax.fori_loop(0, length // TILE, step, (zero, zero, zero))
    for k, part in enumerate(parts):
        sums[k : k + 1, :] = jnp.sum(part, 0, keepdims=True)


def inner_back_kernel(low, w_back, slope, out, sums):
    block = 256
    for i in range(w_back.shape[0] // block):
        cols = slice(i * block, (i + 1) * block)
        value = (nt(low[...], w_back[cols, :]) * slope[:, cols].astype(F32)).astype(BF)
        out[:, cols] = value
        sums[:, cols] = jnp.sum(value.astype(F32), 0, keepdims=True)


def first_back_kernel(inner, w_in, grad_second, n1, r1, g1, w_out, grad, low, att, sums, work):
    length, width = grad_second.shape
    block = 256
    for i in range(width // block):
        cols = slice(i * block, (i + 1) * block)
        work[:, cols] = nt(inner[...], w_in[cols, :])

    def step(i, carry):
        gain_sum, bias_sum, low_sum = carry
        rows = pl.ds(pl.multiple_of(i * TILE, TILE), TILE)
        value = grad_second[rows, :] + work[rows, :]
        normed = n1[rows, :]
        back = norm_back(value, normed, r1[rows, :], g1[...])
        grad[rows, :] = back
        back_low = back.astype(BF)
        low[rows, :] = back_low
        return (
            gain_sum + fold(value * normed),
            bias_sum + fold(value),
            low_sum + fold(back_low.astype(F32)),
        )

    zero = jnp.zeros((8, width), F32)
    parts = lax.fori_loop(0, length // TILE, step, (zero, zero, zero))
    for k, part in enumerate(parts):
        sums[k : k + 1, :] = jnp.sum(part, 0, keepdims=True)
    att[...] = nt(low[...], w_out[...]).astype(BF)


def attention_back_kernel(proj, probs, att_grad, out, sums):
    length = proj.shape[0]
    width = proj.shape[1] // 3
    masks = [head_mask(0), head_mask(1)]
    scale = 1.0 / math.sqrt(HEAD_DIM)
    pair_width = 2 * HEAD_DIM

    def pair_step(pair, carry):
        at = pl.multiple_of(pair * pair_width, pair_width)
        k_at = pl.multiple_of(width + at, pair_width)
        v_at = pl.multiple_of(2 * width + at, pair_width)
        queries = proj[:, pl.ds(at, pair_width)]
        keys = proj[:, pl.ds(k_at, pair_width)]
        values = proj[:, pl.ds(v_at, pair_width)]
        grads = att_grad[:, pl.ds(at, pair_width)]
        grads_t = grads.T
        queries_t = queries.T
        grad_q, grad_k_t, grad_v_t = None, [], []
        for half in range(2):
            low = probs[2 * pair + half]
            wide = low.astype(F32)
            grad_p = nt(grads * masks[half], values)
            delta = jnp.sum(grad_p * wide, -1, keepdims=True)
            grad_s = (wide * (grad_p - delta)).astype(BF)
            lanes = slice(half * HEAD_DIM, (half + 1) * HEAD_DIM)
            grad_v_t.append(nn(grads_t[lanes], low))
            grad_k_t.append(nn(queries_t[lanes], grad_s))
            term = nn(grad_s, keys * masks[half])
            grad_q = term if grad_q is None else grad_q + term
        parts = (
            grad_q * scale,
            jnp.concatenate(grad_k_t, 0).T * scale,
            jnp.concatenate(grad_v_t, 0).T,
        )
        for start, part in zip((at, k_at, v_at), parts):
            part_low = part.astype(BF)
            out[:, pl.ds(start, pair_width)] = part_low
            sums[:, pl.ds(start, pair_width)] = jnp.sum(part_low.astype(F32), 0, keepdims=True)
        return carry

    lax.fori_loop(0, width // pair_width, pair_step, 0)


def input_back_kernel(grad_proj, w_qkv, grad_first, out):
    block = 256
    for i in range(w_qkv.shape[0] // block):
        cols = slice(i * block, (i + 1) * block)
        value = grad_first[:, cols] + nt(grad_proj[...], w_qkv[cols, :])
        out[:, cols] = value.astype(BF)


def slot_device(me, bits, slot):
    mixed = 0
    for b in range(bits):
        mixed = mixed | (((slot >> (bits - 1 - b)) & 1) << b)
    return me ^ mixed


def weight_grad_kernel(place, left, right, keep, send, work, *, bits):
    share = keep.shape[1]
    total = left.shape[1]
    block = min(total, 768)
    for r in range(0, total, block):
        work[r : r + block, :] = tn(left[:, r : r + block], right[...]).astype(BF)
    half = keep.shape[0]
    for slot in range(half):
        for ref, index in ((keep, slot), (send, half + slot)):
            device = slot_device(place[1], bits, index)
            ref[slot] = work[pl.ds(pl.multiple_of(device * share, 16), share), :]


def last_grad_kernel(
    place, x, grad_proj, attended, low, sums_two, sums_one, sums_qkv, sums_in, keep, send, work, *, bits
):
    length, width = x.shape
    share = keep.shape[1]
    wide = grad_proj.shape[1]
    half = keep.shape[0]
    devices = 2 * half
    for part in range(3):
        cols = slice(part * width, (part + 1) * width)
        work[:, cols] = tn(x[...], grad_proj[:, cols]).astype(BF)
    work[:, wide : wide + width] = tn(attended[...], low[...]).astype(BF)
    extra = slice(wide + width, wide + width + 128)
    stacked = jnp.concatenate(
        [sums_qkv[:, :width], sums_qkv[:, 2 * width :], sums_two[0:3], sums_one[0:3]], 0
    )
    work[:, extra] = jnp.zeros((width, 128), BF)
    in_share = sums_in.shape[1] // devices
    for d in range(devices):
        rows = [stacked[:, d * share : (d + 1) * share]]
        for k in range(in_share // share):
            at = d * in_share + k * share
            rows.append(sums_in[:, at : at + share])
        rows.append(jnp.zeros((16 - 8 - in_share // share, share), F32))
        block = jnp.concatenate(rows, 0)
        block = jnp.concatenate([block, jnp.zeros((16, 128 - share), F32)], 1)
        high = block.astype(BF)
        work[d * share : d * share + 16, extra] = high
        work[d * share + 16 : d * share + 32, extra] = (block - high.astype(F32)).astype(BF)
    for slot in range(half):
        for ref, index in ((keep, slot), (send, half + slot)):
            device = slot_device(place[1], bits, index)
            ref[slot] = work[pl.ds(pl.multiple_of(device * share, 16), share), :]


def add_extra(left, right):
    total = (
        left[0:16].astype(F32) + left[16:32].astype(F32) + right[0:16].astype(F32) + right[16:32].astype(F32)
    )
    return total


def halve_kernel(kept, came, keep, send, *, extra):
    half = keep.shape[0]
    cols = keep.shape[2] - extra
    for slot in range(2 * half):
        ref, at = (keep, slot) if slot < half else (send, slot - half)
        ref[at, :, :cols] = (
            kept[slot, :, :cols].astype(F32) + came[slot, :, :cols].astype(F32)
        ).astype(BF)
        if extra:
            total = add_extra(kept[slot, :, cols:], came[slot, :, cols:])
            high = total.astype(BF)
            ref[at, 0:16, cols:] = high
            ref[at, 16:32, cols:] = (total - high.astype(F32)).astype(BF)
            ref[at, 32:, cols:] = jnp.zeros((keep.shape[1] - 32, extra), BF)


def finish_kernel(kept, came, out):
    out[...] = kept[0].astype(F32) + came[0].astype(F32)


def finish_last_kernel(
    kept, came, w_qkv, w_out, bq, bv, gain2, bias2, b_back, gain1, bias1, b_out, b_in
):
    wide, width = w_qkv.shape[1], w_out.shape[1]
    share = bq.shape[1]
    total = kept[0, :, : wide + width].astype(F32) + came[0, :, : wide + width].astype(F32)
    w_qkv[...] = total[:, :wide]
    w_out[...] = total[:, wide:]
    vectors = add_extra(kept[0, :, wide + width :], came[0, :, wide + width :])
    for k, ref in enumerate((bq, bv, gain2, bias2, b_back, gain1, bias1, b_out)):
        ref[...] = vectors[k : k + 1, :share]
    pieces = b_in.shape[1] // share
    b_in[...] = jnp.concatenate([vectors[8 + k : 9 + k, :share] for k in range(pieces)], 1)


def plain_grad_kernel(left, right, out):
    out[...] = tn(left[...], right[...])


def swapped(value, axis, mask):
    count = lax.axis_size(axis)
    return lax.ppermute(value, axis, [(i, i ^ mask) for i in range(count)])


def reduce_shares(keep, send, bits, finish, extra=0):
    for b in range(bits):
        came = swapped(send, "dp", 1 << b)
        if b == bits - 1:
            return finish(keep, came)
        half = keep.shape[0] // 2
        shape = (half,) + keep.shape[1:]
        keep, send = kernel_call(
            functools.partial(halve_kernel, extra=extra),
            [sds(shape, BF), sds(shape, BF)],
            [keep, came],
            mib=8,
            name=f"halve{b}",
        )


def gather_packets(packet, bits):
    count = 1 << bits
    order = [3, 2, 1, 0] if bits == 4 else list(range(bits))
    held = packet[None]
    for b in order:
        held = jnp.concatenate([held, swapped(held, "dp", 1 << b)], 0)
    me = lax.axis_index("dp")
    slots = []
    for s in range(count):
        mixed = 0
        for j, b in enumerate(order):
            mixed |= ((s >> j) & 1) << b
        slots.append(mixed)
    inverse = [0] * count
    for s, mixed in enumerate(slots):
        inverse[mixed] = s
    table = jnp.asarray(inverse, jnp.int32)
    return held[table[jnp.arange(count, dtype=jnp.int32) ^ me]]


def shards(
    hidden_in,
    seg_ids,
    labels,
    out_grad,
    w_qkv,
    b_query,
    b_value,
    w_out,
    b_out,
    ln1_gain,
    ln1_bias,
    w_in,
    b_in,
    w_back,
    b_back,
    ln2_gain,
    ln2_bias,
):
    x, cotangent = hidden_in[0], out_grad[0]
    w_qkv, w_out, w_in, w_back = w_qkv[0], w_out[0], w_in[0], w_back[0]
    length, width = x.shape
    hidden = w_in.shape[1]
    heads = width // HEAD_DIM
    count = length // QLEN
    devices = lax.axis_size("dp")
    bits = devices.bit_length() - 1
    tower, me = lax.axis_index("tower"), lax.axis_index("dp")
    place = jnp.stack([tower, me]).astype(jnp.int32)
    seg_col = seg_ids.reshape(length, 1)
    fast = devices == 16

    proj = kernel_call(
        proj_kernel, sds((length, 3 * width), BF), [x, w_qkv, b_query, b_value],
        mib=16, flops=2 * length * 3 * width * width, name="proj",
    )
    cls = kernel_call(
        cls_kernel, sds((count, width), BF),
        [place, seg_ids, x, proj, w_out, b_out, ln1_gain, ln1_bias, w_in, b_in, w_back, b_back,
         ln2_gain, ln2_bias],
        smem=1, mib=16, flops=2 * 256 * width * hidden * 2, name="cls",
    )
    other = swapped(cls, "tower", 1)
    label_rows = jnp.stack([labels // 256, labels % 256]).astype(F32).astype(BF)
    label_rows = jnp.pad(label_rows, ((0, PACKET - count - SEGS - 2), (0, width - count)))
    q_rows = jnp.where(tower == 0, cls, other)
    p_rows = jnp.where(tower == 0, other, cls)[:SEGS]
    packet = jnp.concatenate([q_rows, p_rows, label_rows], 0)
    if fast:
        packets = gather_packets(packet, bits)
    else:
        packets = lax.all_gather(packet, "dp", axis=0)

    attended, probs = kernel_call(
        attention_kernel, [sds((length, width), BF), sds((heads, length, length), BF)],
        [place, seg_ids, seg_col, proj], smem=1,
        scratch=[pltpu.VMEM((length, length), F32)],
        mib=16, flops=4 * heads * length * length * 256, name="attention",
    )
    work = pltpu.VMEM((length, width), F32)
    n1, r1, first_low = kernel_call(
        first_kernel,
        [sds((length, width), F32), sds((length, 1), F32), sds((length, width), BF)],
        [x, attended, w_out, b_out, ln1_gain, ln1_bias], scratch=[work],
        mib=16, flops=2 * length * width * width, name="first",
    )
    act, slope = kernel_call(
        inner_kernel, [sds((length, hidden), BF), sds((length, hidden), BF)],
        [first_low, w_in, b_in], scratch=[pltpu.VMEM((2, length, 256), F32)],
        mib=16, flops=8 * length * width * hidden, name="inner",
    )
    n2, r2, out_hidden = kernel_call(
        second_kernel,
        [sds((length, width), F32), sds((length, 1), F32), sds((length, width), BF)],
        [act, w_back, b_back, n1, ln1_gain, ln1_bias, ln2_gain, ln2_bias], scratch=[work],
        mib=16, flops=2 * length * width * hidden, name="second",
    )

    queries = packets[:, :count].reshape(devices * count, width)
    passages = packets[:, count : count + SEGS].reshape(devices * SEGS, width)
    label_parts = packets[:, count + SEGS : count + SEGS + 2, :count].astype(jnp.int32)
    all_labels = (label_parts[:, 0] * 256 + label_parts[:, 1]).reshape(devices * count)
    cls_grad = kernel_call(
        loss_kernel, sds((count, width), F32),
        [place, queries, passages, all_labels[None], all_labels[:, None]], smem=1,
        mib=24, flops=8 * devices * count * devices * SEGS * width, name="loss",
    )

    grad_second, second_low, sums_two = kernel_call(
        second_back_kernel,
        [sds((length, width), F32), sds((length, width), BF), sds((8, width), F32)],
        [place, seg_ids, cotangent, cls_grad, n2, r2, ln2_gain], smem=1, scratch=[work],
        mib=16, flops=2 * length * width * 256, name="second_back",
    )

    def weight_grad(left, right, name):
        rows, cols = left.shape[1], right.shape[1]
        flops = 2 * length * rows * cols
        if not fast:
            whole = kernel_call(
                plain_grad_kernel, sds((rows, cols), F32), [left, right], mib=24, flops=flops, name=name
            )
            return lax.psum_scatter(whole, "dp", scatter_dimension=0, tiled=True)
        share = rows // devices
        shape = sds((devices // 2, share, cols), BF)
        keep, send = kernel_call(
            functools.partial(weight_grad_kernel, bits=bits), [shape, shape], [place, left, right],
            smem=1, scratch=[pltpu.VMEM((rows, cols), BF)], mib=24, flops=flops, name=name,
        )
        return reduce_shares(
            keep, send, bits,
            lambda kept, came: kernel_call(
                finish_kernel, sds((share, cols), F32), [kept, came], mib=8, name="finish"
            ),
        )

    share_w_back = weight_grad(act, second_low, "grad_w_back")
    inner_low, sums_in = kernel_call(
        inner_back_kernel, [sds((length, hidden), BF), sds((1, hidden), F32)],
        [second_low, w_back, slope], mib=16, flops=2 * length * width * hidden, name="inner_back",
    )
    share_w_in = weight_grad(first_low, inner_low, "grad_w_in")
    grad_first, branch_low, att_grad, sums_one = kernel_call(
        first_back_kernel,
        [sds((length, width), F32), sds((length, width), BF), sds((length, width), BF), sds((8, width), F32)],
        [inner_low, w_in, grad_second, n1, r1, ln1_gain, w_out], scratch=[work],
        mib=16, flops=2 * length * width * (hidden + width), name="first_back",
    )
    grad_proj, sums_qkv = kernel_call(
        attention_back_kernel, [sds((length, 3 * width), BF), sds((1, 3 * width), F32)],
        [proj, probs, att_grad], mib=16, flops=8 * heads * length * length * 256, name="attention_back",
    )
    if fast:
        share = width // devices
        cols = 4 * width + 128
        shape = sds((devices // 2, share, cols), BF)
        keep, send = kernel_call(
            functools.partial(last_grad_kernel, bits=bits), [shape, shape],
            [place, x, grad_proj, attended, branch_low, sums_two, sums_one, sums_qkv, sums_in],
            smem=1, scratch=[pltpu.VMEM((width, cols), BF)], mib=24,
            flops=8 * length * width * width, name="grad_w_qkv_out",
        )
        small = sds((1, share), F32)
        (
            share_w_qkv, share_w_out, share_bq, share_bv, share_gain2, share_bias2, share_b_back,
            share_gain1, share_bias1, share_b_out, share_b_in,
        ) = reduce_shares(
            keep, send, bits,
            lambda kept, came: kernel_call(
                finish_last_kernel,
                [sds((share, 3 * width), F32), sds((share, width), F32)] + [small] * 8
                + [sds((1, hidden // devices), F32)],
                [kept, came], mib=8, name="finish_last",
            ),
            extra=128,
        )
    else:
        share_w_qkv = weight_grad(x, grad_proj, "grad_w_qkv")
        share_w_out = weight_grad(attended, branch_low, "grad_w_out")

        def scattered(vector):
            return lax.psum_scatter(vector, "dp", scatter_dimension=1, tiled=True)

        share_bq, share_bv = scattered(sums_qkv[:, :width]), scattered(sums_qkv[:, 2 * width :])
        share_gain2, share_bias2, share_b_back = (scattered(sums_two[k : k + 1]) for k in range(3))
        share_gain1, share_bias1, share_b_out = (scattered(sums_one[k : k + 1]) for k in range(3))
        share_b_in = scattered(sums_in)
    grad_hidden = kernel_call(
        input_back_kernel, sds((length, width), BF), [grad_proj, w_qkv, grad_first],
        mib=16, flops=6 * length * width * width, name="input_back",
    )
    return (
        out_hidden[None],
        grad_hidden[None],
        share_w_qkv[None],
        share_bq,
        share_bv,
        share_w_out[None],
        share_b_out,
        share_gain1,
        share_bias1,
        share_w_in[None],
        share_b_in,
        share_w_back[None],
        share_b_back,
        share_gain2,
        share_bias2,
    )


def solution(mesh):
    matrix, vector = P("tower", None, None), P("tower", None)
    rows, spread = P("tower", "dp", None), P("tower", "dp")
    return jax.shard_map(
        shards,
        mesh=mesh,
        in_specs=(
            rows, P("dp", None), P("dp"), rows, matrix, vector, vector, matrix, vector, vector, vector,
            matrix, vector, matrix, vector, vector, vector,
        ),
        out_specs=(
            rows, rows, rows, spread, spread, rows, spread, spread, spread, rows, spread, rows, spread,
            spread, spread,
        ),
        check_vma=False,
    )
```

time: 671 us -> 255 us (0.38); the launches traced: 660 us -> 254 us
  waiting for transfers between devices: 364 us -> 112 us
  matrix products: 116 us -> 0 us
  blocking collectives: 86.7 us -> 0 us
  Pallas kernels: 0 us -> 80.4 us
  other arithmetic: 30.1 us -> 2.28 us
  between operations: 16.5 us -> 1.18 us
  starting transfers between devices: 7.63 us -> 22.8 us
    reduce_scatter x3 -> x0, waiting for transfers between devices: 278 us -> none  [shards(): lax.psum_scatter(ffn_sums + attention_sums, 'dp', scatter_dimension=0, ti...]
    dot_general x23 -> x0, matrix products: 116 us -> none  [the longest x4 27.3 us: contract_rows(): jnp.einsum('ld,le->de', left, right, preferred_element_type=jnp.float32)]
    ppermute x2 -> x17, waiting for transfers between devices: 2.86 us -> 112 us  [swapped(): return lax.ppermute(value, axis, [(i, i ^ mask) for i in range(count)])]
    unnamed x7 -> x0, waiting for transfers between devices: 82.9 us -> none
    pallas_call x0 -> x27, Pallas kernels: none -> 80.4 us  [kernel_call(): pl.pallas_call(body, out_shape=shapes, in_specs=[SM] * smem + [VM] * (len...]
    unnamed x1 -> x0, blocking collectives: 63.4 us -> none
    all_gather x1 -> x0, blocking collectives: 23.3 us -> none  [shards(): lax.all_gather(passage_cls.astype(jnp.bfloat16), 'dp', axis=0, tiled=True)]
    ppermute x2 -> x17, starting transfers between devices: 7.42 us -> 22.8 us  [swapped(): return lax.ppermute(value, axis, [(i, i ^ mask) for i in range(count)])]
  transfers between devices with their start and end apart: 7 -> 17, of which waited for: 5 -> 11; matrix products, arithmetic and copies ran while one was open for 8% -> 1% of each run, Pallas kernels for 0% -> 24%
where the time goes in v1:
time: 255 us; the launch traced here: 254 us
  waiting for transfers between devices  112 us (44%)
  Pallas kernels  80.4 us (32%)
  local copies, waits for them, and re-layouts  35.5 us (14%)
  starting transfers between devices  22.8 us (9%)
    ppermute x17, waiting for transfers between devices, swapped(): return lax.ppermute(value, axis, [(i, i ^ mask) for i in range(count)])  112 us
    pallas_call x27, Pallas kernels, kernel_call(): pl.pallas_call(body, out_shape=shapes, in_specs=[SM] * smem + [VM] * (len...  80.4 us
    unnamed x97, local copies, waits for them, and re-layouts  28.8 us
    ppermute x17, starting transfers between devices, swapped(): return lax.ppermute(value, axis, [(i, i ^ mask) for i in range(count)])  22.8 us
  transfers between devices with their start and end apart: 17, of which 11 were waited for; matrix products, arithmetic and copies ran while one was open for 1% of the time, Pallas kernels for 24%

profile of v1, /device:TPU:0, one launch (start us, length us, event | category | flops | bytes accessed | tf_op | source)
XLA Modules:
  0.0 254.4 jit_solution(16082320182961960816)
XLA Ops:
  0.7 2.0 copy-done.4
  2.7 1.1 copy-done.6
  5.3 2.0 proj.1
  8.0 2.5 copy-done.2
  10.5 3.8 %cls.1 = bf16[16,768]{1,0:T(8,128)(2,1)S(1)} custom-call(s32[2]{0:T(128)S(1)} %pad_add_fusion.place, s32[1,512]{1,0:T(1,128)S(1)} %copy-done.26, bf16[512,768]{1,0:T(8,128)(2,1)S(1)} %bitcast.49, bf16[512,2304]{1,0:T(8,128)(2,1)S(1)} %proj.1, bf16[768,768]{1,0:T(8,128)(2,1)S(1)} %bitcast.43, f32[1,768]{1,0:T(1,128)S(1)} %copy-done.27, ...), custom_call_target="tpu_custom_call" | custom-call | flops 2415919104 | bytes 13819912 | tf_op jit(solution)/shard_map/cls/pallas_call | solution.py:40
  14.3 3.0 %collective-permute-start = (bf16[16,768]{1,0:T(8,128)(2,1)S(1)}, bf16[16,768]{1,0:T(8,128)(2,1)S(1)}, u32[]{:S(2)}, u32[]{:S(2)}) collective-permute-start(bf16[16,768]{1,0:T(8,128)(2,1)S(1)} %cls.1), channel_id=1, source_target_pairs={{0,16},{16,0},{1,17},{17,1},{2,18},{18,2},{3,19},{19,3},{4,20},{20... | collective-permute-start | bytes 73736 | tf_op jit(solution)/shard_map/ppermute | solution.py:501
  17.5 1.7 copy-done.12
  19.2 10.2 %attention.1 = (bf16[512,768]{1,0:T(8,128)(2,1)S(1)}, bf16[12,512,512]{2,1,0:T(8,128)(2,1)S(1)}) custom-call(s32[2]{0:T(128)S(1)} %pad_add_fusion.place, s32[1,512]{1,0:T(1,128)S(1)} %copy-done.26, s32[512,1]{1,0:T(8,128)S(1)} %copy.33.seg_col, bf16[512,2304]{1,0:T(8,128)(2,1)S(1)} %copy-done.12), custom_call_target="tpu_custom_call" | custom-call | flops 3221225472 | bytes 9441288 | tf_op jit(solution)/shard_map/attention/pallas_call | solution.py:40
  29.4 2.6 %copy-done.37 = bf16[12,512,512]{2,1,0:T(8,128)(2,1)} copy-done((bf16[12,512,512]{2,1,0:T(8,128)(2,1)}, bf16[12,512,512]{2,1,0:T(8,128)(2,1)S(1)}, u32[]{:S(2)}) %copy-start.37) | copy-done | bytes 6291480
  32.1 3.9 %first.1 = (f32[512,768]{1,0:T(8,128)S(1)}, f32[512,1]{1,0:T(8,128)S(1)}, bf16[512,768]{1,0:T(8,128)(2,1)S(1)}) custom-call(bf16[512,768]{1,0:T(8,128)(2,1)S(1)} %bitcast.50, bf16[512,768]{1,0:T(8,128)(2,1)S(1)} %get-tuple-element.71.attended, bf16[768,768]{1,0:T(8,128)(2,1)S(1)} %bitcast.44, f32[1,768]{1,0:T(1,128)S(1)} %copy-done.27, ...), custom_call_target="tpu_custom_call" | custom-call | flops 603979776 | bytes 5123072 | tf_op jit(solution)/shard_map/first/pallas_call | solution.py:40
  36.7 7.0 %inner.1 = (bf16[512,3072]{1,0:T(8,128)(2,1)S(1)}, bf16[512,3072]{1,0:T(8,128)(2,1)S(1)}) custom-call(bf16[512,768]{1,0:T(8,128)(2,1)S(1)} %get-tuple-element.72.low.left, bf16[768,3072]{1,0:T(8,128)(2,1)S(1)} %bitcast.39, f32[1,3072]{1,0:T(1,128)S(1)} %copy-done.30), custom_call_target="tpu_custom_call" | custom-call | flops 9663676416 | bytes 11808768 | tf_op jit(solution)/shard_map/inner/pallas_call | solution.py:40
  43.8 1.8 copy-done.35
  45.6 6.7 %second.1 = (f32[512,768]{1,0:T(8,128)S(1)}, f32[512,1]{1,0:T(8,128)S(1)}, bf16[512,768]{1,0:T(8,128)(2,1)}) custom-call(bf16[512,3072]{1,0:T(8,128)(2,1)S(1)} %get-tuple-element.73.act.left, bf16[3072,768]{1,0:T(8,128)(2,1)S(1)} %bitcast.34, f32[1,768]{1,0:T(1,128)S(1)} %copy-done.28, f32[512,768]{1,0:T(8,128)S(1)} %get-tuple-element.74.n1, ...), custom_call_target="tpu_custom_call" | custom-call | flops 2415919104 | bytes 11813888 | tf_op jit(solution)/shard_map/second/pallas_call | solution.py:40
  52.3 1.1 copy-done.14
  54.2 2.7 %collective-permute-start.1 = (bf16[1,24,768]{2,1,0:T(8,128)(2,1)S(1)}, bf16[1,24,768]{2,1,0:T(8,128)(2,1)S(1)}, u32[]{:S(2)}, u32[]{:S(2)}) collective-permute-start(bf16[1,24,768]{2,1,0:T(8,128)(2,1)S(1)} %fusion.2), channel_id=1, source_target_pairs={{0,8},{1,9},{2,10},{3,11},{4,12},{5,13},{6,14},{7,15},{8,0},{9,1},... | collective-permute-start | bytes 110600 | tf_op jit(solution)/shard_map/ppermute | solution.py:501
  57.5 1.6 collective-permute-done.1
  59.1 1.6 collective-permute-start.2
  60.8 2.8 %collective-permute-done.2 = bf16[2,24,768]{2,1,0:T(8,128)(2,1)S(1)} collective-permute-done((bf16[2,24,768]{2,1,0:T(8,128)(2,1)S(1)}, bf16[2,24,768]{2,1,0:T(8,128)(2,1)S(1)}, u32[]{:S(2)}, u32[]{:S(2)}) %collective-permute-start.2) | collective-permute-done | bytes 73760 | tf_op jit(solution)/shard_map/ppermute | solution.py:501
  63.6 1.6 collective-permute-start.3
  65.8 3.0 %collective-permute-done.3 = bf16[4,24,768]{2,1,0:T(8,128)(2,1)S(1)} collective-permute-done((bf16[4,24,768]{2,1,0:T(8,128)(2,1)S(1)}, bf16[4,24,768]{2,1,0:T(8,128)(2,1)S(1)}, u32[]{:S(2)}, u32[]{:S(2)}) %collective-permute-start.3) | collective-permute-done | bytes 147488 | tf_op jit(solution)/shard_map/ppermute | solution.py:501
  71.6 2.5 gather_fusion.1
  75.8 1.0 slice.30
  78.2 2.3 loss.1.cls_grad
  80.5 1.4 copy-done.15
  81.9 1.1 copy-done.16
  84.0 4.4 %second_back.1 = (f32[512,768]{1,0:T(8,128)S(1)}, bf16[512,768]{1,0:T(8,128)(2,1)S(1)}, f32[8,768]{1,0:T(8,128)S(1)}) custom-call(s32[2]{0:T(128)S(1)} %pad_add_fusion.place, s32[1,512]{1,0:T(1,128)S(1)} %copy-done.26, bf16[512,768]{1,0:T(8,128)(2,1)S(1)} %bitcast.53, f32[16,768]{1,0:T(8,128)S(1)} %loss.1.cls_grad, f32[512,768]{1,0:T(8,128)S(1)} %copy-done.15, ...), custom_call_target="tpu_custom_call" | custom-call | flops 201326592 | bytes 4799496 | tf_op jit(solution)/shard_map/second_back/pallas_call | solution.py:40
  88.5 2.3 copy-done.1
  90.8 1.9 copy-done.36
  92.7 2.8 %inner_back.1 = (bf16[512,3072]{1,0:T(8,128)(2,1)S(1)}, f32[1,3072]{1,0:T(1,128)S(1)}) custom-call(bf16[512,768]{1,0:T(8,128)(2,1)S(1)} %get-tuple-element.79.low.right, bf16[3072,768]{1,0:T(8,128)(2,1)S(1)} %bitcast.35, bf16[512,3072]{1,0:T(8,128)(2,1)S(1)} %copy-done.36), custom_call_target="tpu_custom_call" | custom-call | flops 2415919104 | bytes 11808768 | tf_op jit(solution)/shard_map/inner_back/pallas_call | solution.py:40
  95.5 3.5 %grad_w_in.1 = (bf16[8,48,3072]{2,1,0:T(8,128)(2,1)S(1)}, bf16[8,48,3072]{2,1,0:T(8,128)(2,1)S(1)}) custom-call(s32[2]{0:T(128)S(1)} %pad_add_fusion.place, bf16[512,768]{1,0:T(8,128)(2,1)S(1)} %copy-done.32, bf16[512,3072]{1,0:T(8,128)(2,1)S(1)} %get-tuple-element.81.inner.right), custom_call_target="tpu_custom_call" | custom-call | flops 2415919104 | bytes 8650760 | tf_op jit(solution)/shard_map/grad_w_in/pallas_call | solution.py:40
  99.6 6.8 %first_back.1 = (f32[512,768]{1,0:T(8,128)S(1)}, bf16[512,768]{1,0:T(8,128)(2,1)S(1)}, bf16[512,768]{1,0:T(8,128)(2,1)S(1)}, f32[8,768]{1,0:T(8,128)S(1)}) custom-call(bf16[512,3072]{1,0:T(8,128)(2,1)S(1)} %get-tuple-element.81.inner.right, bf16[768,3072]{1,0:T(8,128)(2,1)S(1)} %bitcast.42, f32[512,768]{1,0:T(8,128)S(1)} %get-tuple-element.82.grad_second, ...), custom_call_target="tpu_custom_call" | custom-call | flops 3019898880 | bytes 15365120 | tf_op jit(solution)/shard_map/first_back/pallas_call | solution.py:40
  106.4 2.8 %copy-done.38 = bf16[12,512,512]{2,1,0:T(8,128)(2,1)S(1)} copy-done((bf16[12,512,512]{2,1,0:T(8,128)(2,1)S(1)}, bf16[12,512,512]{2,1,0:T(8,128)(2,1)}, u32[]{:S(2)}) %copy-start.38) | copy-done | bytes 6291480
  109.2 11.4 %attention_back.1 = (bf16[512,2304]{1,0:T(8,128)(2,1)S(1)}, f32[1,2304]{1,0:T(1,128)S(1)}) custom-call(bf16[512,2304]{1,0:T(8,128)(2,1)S(1)} %copy-done.13, bf16[12,512,512]{2,1,0:T(8,128)(2,1)S(1)} %copy-done.38, bf16[512,768]{1,0:T(8,128)(2,1)S(1)} %get-tuple-element.84.att_grad), custom_call_target="tpu_custom_call" | custom-call | flops 6442450944 | bytes 11805696 | tf_op jit(solution)/shard_map/attention_back/pallas_call | solution.py:40
  120.7 3.5 %grad_w_qkv_out.1 = (bf16[8,48,3200]{2,1,0:T(8,128)(2,1)S(1)}, bf16[8,48,3200]{2,1,0:T(8,128)(2,1)S(1)}) custom-call(s32[2]{0:T(128)S(1)} %pad_add_fusion.place, bf16[512,768]{1,0:T(8,128)(2,1)S(1)} %bitcast.51, bf16[512,2304]{1,0:T(8,128)(2,1)S(1)} %get-tuple-element.85.grad_proj, bf16[512,768]{1,0:T(8,128)(2,1)S(1)} %copy-done.18, ...), custom_call_target="tpu_custom_call" | custom-call | flops 2415919104 | bytes 9704456 | tf_op jit(solution)/shard_map/grad_w_qkv_out/pallas_call | solution.py:40
  124.3 3.5 %grad_w_back.1 = (bf16[8,192,768]{2,1,0:T(8,128)(2,1)S(1)}, bf16[8,192,768]{2,1,0:T(8,128)(2,1)S(1)}) custom-call(s32[2]{0:T(128)S(1)} %pad_add_fusion.place, bf16[512,3072]{1,0:T(8,128)(2,1)S(1)} %copy-done.10, bf16[512,768]{1,0:T(8,128)(2,1)S(1)} %get-tuple-element.79.low.right), custom_call_target="tpu_custom_call" | custom-call | flops 2415919104 | bytes 8650760 | tf_op jit(solution)/shard_map/grad_w_back/pallas_call | solution.py:40
  129.5 1.6 collective-permute-start.6
  133.1 1.6 collective-permute-start.14
  134.7 24.8 %collective-permute-done.6.came = bf16[4,48,3200]{2,1,0:T(8,128)(2,1)S(1)} collective-permute-done((bf16[4,48,3200]{2,1,0:T(8,128)(2,1)S(1)}, bf16[4,48,3200]{2,1,0:T(8,128)(2,1)S(1)}, u32[]{:S(2)}, u32[]{:S(2)}) %collective-permute-start.6) | collective-permute-done | bytes 1228832 | tf_op jit(solution)/shard_map/ppermute | solution.py:501
  159.7 1.6 collective-permute-start.7
  161.4 23.4 %collective-permute-done.10.came = bf16[4,48,3072]{2,1,0:T(8,128)(2,1)S(1)} collective-permute-done((bf16[4,48,3072]{2,1,0:T(8,128)(2,1)S(1)}, bf16[4,48,3072]{2,1,0:T(8,128)(2,1)S(1)}, u32[]{:S(2)}, u32[]{:S(2)}) %collective-permute-start.10) | collective-permute-done | bytes 1179680 | tf_op jit(solution)/shard_map/ppermute | solution.py:501
  185.0 1.6 collective-permute-start.11
  186.7 22.6 %collective-permute-done.14.came = bf16[4,192,768]{2,1,0:T(8,128)(2,1)S(1)} collective-permute-done((bf16[4,192,768]{2,1,0:T(8,128)(2,1)S(1)}, bf16[4,192,768]{2,1,0:T(8,128)(2,1)S(1)}, u32[]{:S(2)}, u32[]{:S(2)}) %collective-permute-start.14) | collective-permute-done | bytes 1179680 | tf_op jit(solution)/shard_map/ppermute | solution.py:501
  209.5 1.6 collective-permute-start.15
  211.3 2.9 %collective-permute-start.8 = (bf16[1,48,3200]{2,1,0:T(8,128)(2,1)S(1)}, bf16[1,48,3200]{2,1,0:T(8,128)(2,1)S(1)}, u32[]{:S(2)}, u32[]{:S(2)}) collective-permute-start(bf16[1,48,3200]{2,1,0:T(8,128)(2,1)S(1)} %get-tuple-element.99), channel_id=1, source_target_pairs={{0,8},{1,9},{2,10},{3,11},{4,12},{5,13},{6,14},{7,15},{8,0},{9,1},... | collective-permute-start | bytes 921608 | tf_op jit(solution)/shard_map/ppermute | solution.py:501
  214.5 21.8 %collective-permute-done.15.came = bf16[2,192,768]{2,1,0:T(8,128)(2,1)S(1)} collective-permute-done((bf16[2,192,768]{2,1,0:T(8,128)(2,1)S(1)}, bf16[2,192,768]{2,1,0:T(8,128)(2,1)S(1)}, u32[]{:S(2)}, u32[]{:S(2)}) %collective-permute-start.15) | collective-permute-done | bytes 589856 | tf_op jit(solution)/shard_map/ppermute | solution.py:501
  237.3 2.9 %input_back.1 = bf16[512,768]{1,0:T(8,128)(2,1)} custom-call(bf16[512,2304]{1,0:T(8,128)(2,1)S(1)} %get-tuple-element.85.grad_proj, bf16[768,2304]{1,0:T(8,128)(2,1)S(1)} %bitcast.47, f32[512,768]{1,0:T(8,128)S(1)} %get-tuple-element.86.grad_first), custom_call_target="tpu_custom_call" | custom-call | flops 1811939328 | bytes 8257536 | tf_op jit(solution)/shard_map/input_back/pallas_call | solution.py:40
  240.2 6.7 %collective-permute-done.12.came = bf16[1,48,3072]{2,1,0:T(8,128)(2,1)S(1)} collective-permute-done((bf16[1,48,3072]{2,1,0:T(8,128)(2,1)S(1)}, bf16[1,48,3072]{2,1,0:T(8,128)(2,1)S(1)}, u32[]{:S(2)}, u32[]{:S(2)}) %collective-permute-start.12) | collective-permute-done | bytes 294944 | tf_op jit(solution)/shard_map/ppermute | solution.py:501
  247.8 4.8 %collective-permute-done.16.came = bf16[1,192,768]{2,1,0:T(8,128)(2,1)S(1)} collective-permute-done((bf16[1,192,768]{2,1,0:T(8,128)(2,1)S(1)}, bf16[1,192,768]{2,1,0:T(8,128)(2,1)S(1)}, u32[]{:S(2)}, u32[]{:S(2)}) %collective-permute-start.16) | collective-permute-done | bytes 294944 | tf_op jit(solution)/shard_map/ppermute | solution.py:501
  (139 shorter events, 21.2 us)
Async XLA Ops:
  5.2 2.7 %copy-start.3 = (bf16[1,768,768]{2,1,0:T(8,128)(2,1)S(1)}, bf16[1,768,768]{2,1,0:T(8,128)(2,1)}, u32[]{:S(2)}) copy-start(bf16[1,768,768]{2,1,0:T(8,128)(2,1)} %param.25) | copy-start | bytes 3538948
  5.2 2.7 %copy-start.23 = (f32[1,768]{1,0:T(1,128)S(1)}, f32[1,768]{1,0:T(1,128)}, u32[]{:S(2)}) copy-start(f32[1,768]{1,0:T(1,128)} %g1.7) | copy-start | bytes 9220
  5.2 2.7 %copy-start.24 = (f32[1,768]{1,0:T(1,128)S(1)}, f32[1,768]{1,0:T(1,128)}, u32[]{:S(2)}) copy-start(f32[1,768]{1,0:T(1,128)} %b1.5) | copy-start | bytes 9220
  5.2 2.7 %copy-start.25 = (f32[1,768]{1,0:T(1,128)S(1)}, f32[1,768]{1,0:T(1,128)}, u32[]{:S(2)}) copy-start(f32[1,768]{1,0:T(1,128)} %g2.5) | copy-start | bytes 9220
  5.3 2.7 %copy-start.26 = (s32[1,512]{1,0:T(1,128)S(1)}, s32[1,512]{1,0:T(1,128)}, u32[]{:S(2)}) copy-start(s32[1,512]{1,0:T(1,128)} %seg.3) | copy-start | bytes 6148
  5.3 2.7 %copy-start.27 = (f32[1,768]{1,0:T(1,128)S(1)}, f32[1,768]{1,0:T(1,128)}, u32[]{:S(2)}) copy-start(f32[1,768]{1,0:T(1,128)} %b_out.3) | copy-start | bytes 9220
  5.3 2.7 %copy-start.28 = (f32[1,768]{1,0:T(1,128)S(1)}, f32[1,768]{1,0:T(1,128)}, u32[]{:S(2)}) copy-start(f32[1,768]{1,0:T(1,128)} %b_back.3) | copy-start | bytes 9220
  5.3 2.7 %copy-start.29 = (f32[1,768]{1,0:T(1,128)S(1)}, f32[1,768]{1,0:T(1,128)}, u32[]{:S(2)}) copy-start(f32[1,768]{1,0:T(1,128)} %b2.3) | copy-start | bytes 9220
  5.3 2.7 %copy-start.30 = (f32[1,3072]{1,0:T(1,128)S(1)}, f32[1,3072]{1,0:T(1,128)}, u32[]{:S(2)}) copy-start(f32[1,3072]{1,0:T(1,128)} %b_in.3) | copy-start | bytes 36868
  7.3 7.0 %copy-start.11 = (bf16[512,2304]{1,0:T(8,128)(2,1)}, bf16[512,2304]{1,0:T(8,128)(2,1)S(1)}, u32[]{:S(2)}) copy-start(bf16[512,2304]{1,0:T(8,128)(2,1)S(1)} %proj.1) | copy-start | bytes 7077892
  10.5 6.9 %copy-start.40 = (s32[16]{0:T(128)S(1)}, s32[16]{0:T(128)}, u32[]{:S(2)}) copy-start(s32[16]{0:T(128)} %param.20) | copy-start | bytes 196
  10.5 26.2 %slice-start.2 = ((s8[4718592]{0:T(1024)(128)(4,1)}), s8[524288]{0:T(1024)(128)(4,1)S(1)}, s32[]{:S(2)}) async-start(s8[4718592]{0:T(1024)(128)(4,1)} %bitcast.37), calls=%async_computation.2 | async-start | bytes 1048576
  14.3 39.9 %collective-permute-start = (bf16[16,768]{1,0:T(8,128)(2,1)S(1)}, bf16[16,768]{1,0:T(8,128)(2,1)S(1)}, u32[]{:S(2)}, u32[]{:S(2)}) collective-permute-start(bf16[16,768]{1,0:T(8,128)(2,1)S(1)} %cls.1), channel_id=1, source_target_pairs={{0,16},{16,0},{1,17},{17,1},{2,18},{18,2},{3,19},{19,3},{4,20},{20... | collective-permute-start | bytes 73736 | tf_op jit(solution)/shard_map/ppermute | solution.py:501
  19.2 12.9 %copy-start.7 = (bf16[1,512,768]{2,1,0:T(8,128)(2,1)S(1)}, bf16[1,512,768]{2,1,0:T(8,128)(2,1)}, u32[]{:S(2)}) copy-start(bf16[1,512,768]{2,1,0:T(8,128)(2,1)} %param.18) | copy-start | bytes 2359300
  19.2 17.5 %slice-start.3 = ((s8[4718592]{0:T(1024)(128)(4,1)}), s8[4194304]{0:T(1024)(128)(4,1)S(1)}, s32[]{:S(2)}) async-start(s8[4718592]{0:T(1024)(128)(4,1)} %bitcast.37), calls=%async_computation.3 | async-start | bytes 8388608
  29.4 2.6 %copy-start.37 = (bf16[12,512,512]{2,1,0:T(8,128)(2,1)}, bf16[12,512,512]{2,1,0:T(8,128)(2,1)S(1)}, u32[]{:S(2)}) copy-start(bf16[12,512,512]{2,1,0:T(8,128)(2,1)S(1)} %get-tuple-element.76.probs) | copy-start | bytes 18874372
  32.0 3.9 %copy-start.17 = (bf16[512,768]{1,0:T(8,128)(2,1)}, bf16[512,768]{1,0:T(8,128)(2,1)S(1)}, u32[]{:S(2)}) copy-start(bf16[512,768]{1,0:T(8,128)(2,1)S(1)} %get-tuple-element.71.attended) | copy-start | bytes 2359300
  32.0 13.5 %slice-start = ((s8[4718592]{0:T(1024)(128)(4,1)}), s8[4194304]{0:T(1024)(128)(4,1)S(1)}, s32[]{:S(2)}) async-start(s8[4718592]{0:T(1024)(128)(4,1)} %bitcast.32), calls=%async_computation | async-start | bytes 8388608
  36.7 7.1 %copy-start.31 = (bf16[512,768]{1,0:T(8,128)(2,1)}, bf16[512,768]{1,0:T(8,128)(2,1)S(1)}, u32[]{:S(2)}) copy-start(bf16[512,768]{1,0:T(8,128)(2,1)S(1)} %get-tuple-element.72.low.left) | copy-start | bytes 2359300
  36.7 8.9 %slice-start.1 = ((s8[4718592]{0:T(1024)(128)(4,1)}), s8[524288]{0:T(1024)(128)(4,1)S(1)}, s32[]{:S(2)}) async-start(s8[4718592]{0:T(1024)(128)(4,1)} %bitcast.32), calls=%async_computation.1 | async-start | bytes 1048576
  45.6 6.7 %copy-start.9 = (bf16[512,3072]{1,0:T(8,128)(2,1)}, bf16[512,3072]{1,0:T(8,128)(2,1)S(1)}, u32[]{:S(2)}) copy-start(bf16[512,3072]{1,0:T(8,128)(2,1)S(1)} %get-tuple-element.73.act.left) | copy-start | bytes 9437188
  45.6 11.3 %copy-start.39 = (s32[16]{0:T(128)S(1)}, s32[16]{0:T(128)}, u32[]{:S(2)}) copy-start(s32[16]{0:T(128)} %constant.46.clone) | copy-start | bytes 196
  54.2 4.9 %collective-permute-start.1 = (bf16[1,24,768]{2,1,0:T(8,128)(2,1)S(1)}, bf16[1,24,768]{2,1,0:T(8,128)(2,1)S(1)}, u32[]{:S(2)}, u32[]{:S(2)}) collective-permute-start(bf16[1,24,768]{2,1,0:T(8,128)(2,1)S(1)} %fusion.2), channel_id=1, source_target_pairs={{0,8},{1,9},{2,10},{3,11},{4,12},{5,13},{6,14},{7,15},{8,0},{9,1},... | collective-permute-start | bytes 110600 | tf_op jit(solution)/shard_map/ppermute | solution.py:501
  59.1 4.4 %collective-permute-start.2 = (bf16[2,24,768]{2,1,0:T(8,128)(2,1)S(1)}, bf16[2,24,768]{2,1,0:T(8,128)(2,1)S(1)}, u32[]{:S(2)}, u32[]{:S(2)}) collective-permute-start(bf16[2,24,768]{2,1,0:T(8,128)(2,1)S(1)} %pad_maximum_fusion.2), channel_id=1, source_target_pairs={{0,4},{1,5},{2,6},{3,7},{4,0},{5,1},{6,2},{7,3},{8,12},{9,13},{10,... | collective-permute-start | bytes 221192 | tf_op jit(solution)/shard_map/ppermute | solution.py:501
  63.6 5.2 %collective-permute-start.3 = (bf16[4,24,768]{2,1,0:T(8,128)(2,1)S(1)}, bf16[4,24,768]{2,1,0:T(8,128)(2,1)S(1)}, u32[]{:S(2)}, u32[]{:S(2)}) collective-permute-start(bf16[4,24,768]{2,1,0:T(8,128)(2,1)S(1)} %pad_maximum_fusion.1), channel_id=1, source_target_pairs={{0,2},{1,3},{2,0},{3,1},{4,6},{5,7},{6,4},{7,5},{8,10},{9,11},{10,... | collective-permute-start | bytes 442376 | tf_op jit(solution)/shard_map/ppermute | solution.py:501
  68.8 2.0 collective-permute-start.4
  92.7 2.8 %copy-start.32 = (bf16[512,768]{1,0:T(8,128)(2,1)S(1)}, bf16[512,768]{1,0:T(8,128)(2,1)}, u32[]{:S(2)}) copy-start(bf16[512,768]{1,0:T(8,128)(2,1)} %copy-done.31) | copy-start | bytes 2359300
  92.7 6.9 %slice-start.4 = ((s8[4718592]{0:T(1024)(128)(4,1)}), s8[4194304]{0:T(1024)(128)(4,1)S(1)}, s32[]{:S(2)}) async-start(s8[4718592]{0:T(1024)(128)(4,1)} %bitcast.40), calls=%async_computation.4 | async-start | bytes 8388608
  95.5 4.1 %slice-start.5 = ((s8[4718592]{0:T(1024)(128)(4,1)}), s8[524288]{0:T(1024)(128)(4,1)S(1)}, s32[]{:S(2)}) async-start(s8[4718592]{0:T(1024)(128)(4,1)} %bitcast.40), calls=%async_computation.5 | async-start | bytes 1048576
  95.5 4.1 %copy-start.20 = (f32[512,1]{1,0:T(8,128)S(1)}, f32[512,1]{1,0:T(8,128)}, u32[]{:S(2)}) copy-start(f32[512,1]{1,0:T(8,128)} %copy-done.19) | copy-start | bytes 6148
  99.0 32.1 %collective-permute-start.9 = (bf16[8,48,3072]{2,1,0:T(8,128)(2,1)S(1)}, bf16[8,48,3072]{2,1,0:T(8,128)(2,1)S(1)}, u32[]{:S(2)}, u32[]{:S(2)}) collective-permute-start(bf16[8,48,3072]{2,1,0:T(8,128)(2,1)S(1)} %get-tuple-element.108), channel_id=1, source_target_pairs={{0,1},{1,0},{2,3},{3,2},{4,5},{5,4},{6,7},{7,6},{8,9},{9,8},{10,11... | collective-permute-start | bytes 7077896 | tf_op jit(solution)/shard_map/ppermute | solution.py:501
  99.6 6.8 %copy-start.13 = (bf16[512,2304]{1,0:T(8,128)(2,1)S(1)}, bf16[512,2304]{1,0:T(8,128)(2,1)}, u32[]{:S(2)}) copy-start(bf16[512,2304]{1,0:T(8,128)(2,1)} %copy-done.11) | copy-start | bytes 7077892
  106.4 2.8 %copy-start.38 = (bf16[12,512,512]{2,1,0:T(8,128)(2,1)S(1)}, bf16[12,512,512]{2,1,0:T(8,128)(2,1)}, u32[]{:S(2)}) copy-start(bf16[12,512,512]{2,1,0:T(8,128)(2,1)} %copy-done.37) | copy-start | bytes 18874372
  109.2 11.4 %copy-start.8 = (bf16[1,512,768]{2,1,0:T(8,128)(2,1)S(1)}, bf16[1,512,768]{2,1,0:T(8,128)(2,1)}, u32[]{:S(2)}) copy-start(bf16[1,512,768]{2,1,0:T(8,128)(2,1)} %param.18) | copy-start | bytes 2359300
  109.2 11.4 %copy-start.18 = (bf16[512,768]{1,0:T(8,128)(2,1)S(1)}, bf16[512,768]{1,0:T(8,128)(2,1)}, u32[]{:S(2)}) copy-start(bf16[512,768]{1,0:T(8,128)(2,1)} %copy-done.17) | copy-start | bytes 2359300
  120.7 3.7 %copy-start.10 = (bf16[512,3072]{1,0:T(8,128)(2,1)S(1)}, bf16[512,3072]{1,0:T(8,128)(2,1)}, u32[]{:S(2)}) copy-start(bf16[512,3072]{1,0:T(8,128)(2,1)} %copy-done.9) | copy-start | bytes 9437188
  124.2 4.7 %collective-permute-start.5 = (bf16[8,48,3200]{2,1,0:T(8,128)(2,1)S(1)}, bf16[8,48,3200]{2,1,0:T(8,128)(2,1)S(1)}, u32[]{:S(2)}, u32[]{:S(2)}) collective-permute-start(bf16[8,48,3200]{2,1,0:T(8,128)(2,1)S(1)} %get-tuple-element.93), channel_id=1, source_target_pairs={{0,1},{1,0},{2,3},{3,2},{4,5},{5,4},{6,7},{7,6},{8,9},{9,8},{10,11... | collective-permute-start | bytes 7372808 | tf_op jit(solution)/shard_map/ppermute | solution.py:501
  127.8 4.7 %collective-permute-start.13 = (bf16[8,192,768]{2,1,0:T(8,128)(2,1)S(1)}, bf16[8,192,768]{2,1,0:T(8,128)(2,1)S(1)}, u32[]{:S(2)}, u32[]{:S(2)}) collective-permute-start(bf16[8,192,768]{2,1,0:T(8,128)(2,1)S(1)} %get-tuple-element.117), channel_id=1, source_target_pairs={{0,1},{1,0},{2,3},{3,2},{4,5},{5,4},{6,7},{7,6},{8,9},{9,8},{10,11... | collective-permute-start | bytes 7077896 | tf_op jit(solution)/shard_map/ppermute | solution.py:501
  129.5 29.9 %collective-permute-start.6 = (bf16[4,48,3200]{2,1,0:T(8,128)(2,1)S(1)}, bf16[4,48,3200]{2,1,0:T(8,128)(2,1)S(1)}, u32[]{:S(2)}, u32[]{:S(2)}) collective-permute-start(bf16[4,48,3200]{2,1,0:T(8,128)(2,1)S(1)} %get-tuple-element.95), channel_id=1, source_target_pairs={{0,2},{1,3},{2,0},{3,1},{4,6},{5,7},{6,4},{7,5},{8,10},{9,11},{10,... | collective-permute-start | bytes 3686408 | tf_op jit(solution)/shard_map/ppermute | solution.py:501
  131.6 53.1 %collective-permute-start.10 = (bf16[4,48,3072]{2,1,0:T(8,128)(2,1)S(1)}, bf16[4,48,3072]{2,1,0:T(8,128)(2,1)S(1)}, u32[]{:S(2)}, u32[]{:S(2)}) collective-permute-start(bf16[4,48,3072]{2,1,0:T(8,128)(2,1)S(1)} %get-tuple-element.110), channel_id=1, source_target_pairs={{0,2},{1,3},{2,0},{3,1},{4,6},{5,7},{6,4},{7,5},{8,10},{9,11},{10,... | collective-permute-start | bytes 3538952 | tf_op jit(solution)/shard_map/ppermute | solution.py:501
  133.1 76.1 %collective-permute-start.14 = (bf16[4,192,768]{2,1,0:T(8,128)(2,1)S(1)}, bf16[4,192,768]{2,1,0:T(8,128)(2,1)S(1)}, u32[]{:S(2)}, u32[]{:S(2)}) collective-permute-start(bf16[4,192,768]{2,1,0:T(8,128)(2,1)S(1)} %get-tuple-element.119), channel_id=1, source_target_pairs={{0,2},{1,3},{2,0},{3,1},{4,6},{5,7},{6,4},{7,5},{8,10},{9,11},{10,... | collective-permute-start | bytes 3538952 | tf_op jit(solution)/shard_map/ppermute | solution.py:501
  159.7 51.4 %collective-permute-start.7 = (bf16[2,48,3200]{2,1,0:T(8,128)(2,1)S(1)}, bf16[2,48,3200]{2,1,0:T(8,128)(2,1)S(1)}, u32[]{:S(2)}, u32[]{:S(2)}) collective-permute-start(bf16[2,48,3200]{2,1,0:T(8,128)(2,1)S(1)} %get-tuple-element.97), channel_id=1, source_target_pairs={{0,4},{1,5},{2,6},{3,7},{4,0},{5,1},{6,2},{7,3},{8,12},{9,13},{10,... | collective-permute-start | bytes 1843208 | tf_op jit(solution)/shard_map/ppermute | solution.py:501
  185.0 29.2 %collective-permute-start.11 = (bf16[2,48,3072]{2,1,0:T(8,128)(2,1)S(1)}, bf16[2,48,3072]{2,1,0:T(8,128)(2,1)S(1)}, u32[]{:S(2)}, u32[]{:S(2)}) collective-permute-start(bf16[2,48,3072]{2,1,0:T(8,128)(2,1)S(1)} %get-tuple-element.112), channel_id=1, source_target_pairs={{0,4},{1,5},{2,6},{3,7},{4,0},{5,1},{6,2},{7,3},{8,12},{9,13},{10,... | collective-permute-start | bytes 1769480 | tf_op jit(solution)/shard_map/ppermute | solution.py:501
  209.5 27.8 %copy-start.5 = (bf16[1,768,2304]{2,1,0:T(8,128)(2,1)S(1)}, bf16[1,768,2304]{2,1,0:T(8,128)(2,1)}, u32[]{:S(2)}) copy-start(bf16[1,768,2304]{2,1,0:T(8,128)(2,1)} %param.22) | copy-start | bytes 10616836
  209.5 26.8 %collective-permute-start.15 = (bf16[2,192,768]{2,1,0:T(8,128)(2,1)S(1)}, bf16[2,192,768]{2,1,0:T(8,128)(2,1)S(1)}, u32[]{:S(2)}, u32[]{:S(2)}) collective-permute-start(bf16[2,192,768]{2,1,0:T(8,128)(2,1)S(1)} %get-tuple-element.121), channel_id=1, source_target_pairs={{0,4},{1,5},{2,6},{3,7},{4,0},{5,1},{6,2},{7,3},{8,12},{9,13},{10,... | collective-permute-start | bytes 1769480 | tf_op jit(solution)/shard_map/ppermute | solution.py:501
  211.3 42.2 %collective-permute-start.8 = (bf16[1,48,3200]{2,1,0:T(8,128)(2,1)S(1)}, bf16[1,48,3200]{2,1,0:T(8,128)(2,1)S(1)}, u32[]{:S(2)}, u32[]{:S(2)}) collective-permute-start(bf16[1,48,3200]{2,1,0:T(8,128)(2,1)S(1)} %get-tuple-element.99), channel_id=1, source_target_pairs={{0,8},{1,9},{2,10},{3,11},{4,12},{5,13},{6,14},{7,15},{8,0},{9,1},... | collective-permute-start | bytes 921608 | tf_op jit(solution)/shard_map/ppermute | solution.py:501
  214.4 32.6 %collective-permute-start.12 = (bf16[1,48,3072]{2,1,0:T(8,128)(2,1)S(1)}, bf16[1,48,3072]{2,1,0:T(8,128)(2,1)S(1)}, u32[]{:S(2)}, u32[]{:S(2)}) collective-permute-start(bf16[1,48,3072]{2,1,0:T(8,128)(2,1)S(1)} %get-tuple-element.114), channel_id=1, source_target_pairs={{0,8},{1,9},{2,10},{3,11},{4,12},{5,13},{6,14},{7,15},{8,0},{9,1},... | collective-permute-start | bytes 884744 | tf_op jit(solution)/shard_map/ppermute | solution.py:501
  236.4 16.2 %collective-permute-start.16 = (bf16[1,192,768]{2,1,0:T(8,128)(2,1)S(1)}, bf16[1,192,768]{2,1,0:T(8,128)(2,1)S(1)}, u32[]{:S(2)}, u32[]{:S(2)}) collective-permute-start(bf16[1,192,768]{2,1,0:T(8,128)(2,1)S(1)} %get-tuple-element.123), channel_id=1, source_target_pairs={{0,8},{1,9},{2,10},{3,11},{4,12},{5,13},{6,14},{7,15},{8,0},{9,1},... | collective-permute-start | bytes 884744 | tf_op jit(solution)/shard_map/ppermute | solution.py:501
  (16 other events, 23.1 us)
